TPU v7x, 256 devices: a whole 4x4x8 slice. The times are simulated.
256 devices in a mesh: tm: 16 (over x, y), rows: 16 (over z, core).
Axes of the slice: x: 4, y: 4, z: 8, core: 2. Of those that a mesh axis runs over, the one named last changes fastest.
Arguments:
- latents: bfloat16 [128, 64, 64, 256], P('tm', 'rows'), may hold values from -6 to 6
- cotangent: bfloat16 [128, 64, 64, 256], P('tm', 'rows'), may hold values from -6 to 6
- w_spatial: bfloat16 [9, 256, 256], replicated, may hold values from -0.125 to 0.125
- w_time: bfloat16 [4, 2, 256, 256], replicated, may hold values from -0.25 to 0.25
Outputs:
- block_out: bfloat16 [128, 64, 64, 256], P('tm', 'rows')
- input_grad: bfloat16 [128, 64, 64, 256], P('tm', 'rows')
- spatial_grad: float32 [9, 256, 256], P(None, None, 'rows')
- time_grad: float32 [4, 2, 256, 256], P(None, None, None, 'rows')
All inputs are finite; a program needn't handle non-finite values.
Results may differ from a plain program's by a relative error of at most 0.013.
Values may be sent and summed in bfloat16 or wider, within the bound.
A program may use at most 128 MiB of HBM per device.

v0:
```python
import math

import jax
import jax.numpy as jnp
from jax import lax
from jax.sharding import PartitionSpec as P


def with_halo(block, sides, width):
    for axis, dim in sides:
        count = lax.axis_size(axis)
        forward = [(i, i + 1) for i in range(count - 1)]
        backward = [(target, source) for source, target in forward]
        low = lax.ppermute(
            lax.slice_in_dim(block, block.shape[dim] - width, None, axis=dim), axis, forward
        )
        high = lax.ppermute(lax.slice_in_dim(block, 0, width, axis=dim), axis, backward)
        block = jnp.concatenate([low, block, high], axis=dim)
    return block


def passed_along(block, axis, distance):
    devices = range(lax.axis_size(axis))
    route = [(i - distance, i) for i in devices if i - distance in devices]
    return lax.ppermute(block, axis, route)


def project(values, weight):
    flat = values.reshape(-1, values.shape[-1])
    return jnp.dot(flat, weight, preferred_element_type=jnp.float32).reshape(
        values.shape[:-1] + (weight.shape[-1],)
    )


def project_back(values, weight):
    flat = values.reshape(-1, values.shape[-1])
    result = lax.dot_general(
        flat, weight, (((1,), (1,)), ((), ())), preferred_element_type=jnp.float32
    )
    return result.reshape(values.shape[:-1] + (weight.shape[0],))


def contract_rows(left, right):
    left_flat = left.reshape(-1, left.shape[-1])
    right_flat = right.reshape(-1, right.shape[-1])
    return lax.dot_general(
        left_flat, right_flat, (((0,), (0,)), ((), ())), preferred_element_type=jnp.float32
    )


def silu_slope(values):
    sigma = jax.nn.sigmoid(values)
    return sigma * (1.0 + values * (1.0 - sigma))


def shards(latents, cotangent, w_spatial, w_time):
    frames = latents.shape[0]
    height = latents.shape[1]
    width = latents.shape[2]
    bordered = with_halo(latents, (("rows", 1),), 1)
    padded = jnp.pad(bordered, ((0, 0), (0, 0), (1, 1), (0, 0)))
    preact = jnp.zeros(latents.shape, jnp.float32)
    for shift_row in range(3):
        for shift_col in range(3):
            window = padded[:, shift_row : shift_row + height, shift_col : shift_col + width]
            preact = preact + project(window, w_spatial[3 * shift_row + shift_col])
    state = jax.nn.silu(preact).astype(jnp.bfloat16)
    states = []
    delayed = []
    temporals = []
    for layer in range(4):
        dilation = 2**layer
        earlier = passed_along(state[frames - dilation :], "tm", 1)
        lagged = jnp.concatenate([earlier, state[: frames - dilation]], axis=0)
        states.append(state)
        delayed.append(lagged)
        temporal = project(state, w_time[layer, 0]) + project(lagged, w_time[layer, 1])
        temporals.append(temporal)
        if layer < 3:
            state = jax.nn.silu(temporal).astype(jnp.bfloat16)
    block_out = (latents.astype(jnp.float32) + temporal).astype(jnp.bfloat16)
    positions = frames * lax.axis_size("tm") * height * lax.axis_size("rows") * width
    factor = 1.0 / math.sqrt(positions)
    delta = cotangent
    time_parts = [None] * 4
    for layer in range(3, -1, -1):
        dilation = 2**layer
        grad_now = contract_rows(states[layer], delta)
        grad_past = contract_rows(delayed[layer], delta)
        time_parts[layer] = jnp.stack([grad_now, grad_past])
        arrival = passed_along(delta[:dilation], "tm", -1)
        advanced = jnp.concatenate([delta[dilation:], arrival], axis=0)
        back = project_back(delta, w_time[layer, 0]) + project_back(advanced, w_time[layer, 1])
        if layer > 0:
            delta = (back * silu_slope(temporals[layer - 1])).astype(jnp.bfloat16)
        else:
            spatial_delta = (back * silu_slope(preact)).astype(jnp.bfloat16)
    time_total = jnp.stack(time_parts)
    delta_rim = with_halo(spatial_delta, (("rows", 1),), 1)
    padded_delta = jnp.pad(delta_rim, ((0, 0), (0, 0), (1, 1), (0, 0)))
    input_grad = cotangent.astype(jnp.float32)
    spatial_parts = []
    for shift_row in range(3):
        for shift_col in range(3):
            kernel = w_spatial[3 * shift_row + shift_col]
            window = padded[:, shift_row : shift_row + height, shift_col : shift_col + width]
            spatial_parts.append(contract_rows(window, spatial_delta))
            source = padded_delta[
                :, 2 - shift_row : 2 - shift_row + height, 2 - shift_col : 2 - shift_col + width
            ]
            input_grad = input_grad + project_back(source, kernel)
    spatial_total = jnp.stack(spatial_parts)
    summed = lax.psum((spatial_total, time_total), "tm")
    spatial_share, time_share = (
        lax.psum_scatter(summed[0], "rows", scatter_dimension=2, tiled=True),
        lax.psum_scatter(summed[1], "rows", scatter_dimension=3, tiled=True),
    )
    return (block_out, input_grad.astype(jnp.bfloat16), spatial_share * factor, time_share * factor)


def solution(mesh):
    in_specs = (P("tm", "rows", None, None), P("tm", "rows", None, None), P(), P())
    out_specs = (
        P("tm", "rows", None, None),
        P("tm", "rows", None, None),
        P(None, None, "rows"),
        P(None, None, None, "rows"),
    )
    return jax.shard_map(shards, mesh=mesh, in_specs=in_specs, out_specs=out_specs, check_vma=False)
```

profile of v0, /device:TPU:1, one launch (start us, length us, event | category | flops | bytes accessed | tf_op | source)
XLA Modules:
  0.0 405.3 jit_solution(16670115501324063130)
XLA Ops:
  8.4 4.9 %collective-permute-start = (bf16[8,1,64,256]{3,2,1,0:T(8,128)(2,1)S(1)}, bf16[8,1,64,256]{3,2,1,0:T(8,128)(2,1)S(1)}, u32[]{:S(2)}, u32[]{:S(2)}) collective-permute-start(bf16[8,1,64,256]{3,2,1,0:T(8,128)(2,1)S(1)} %get-tuple-element.22), channel_id=1, source_target_pairs={{0,1},{1,2},{2,3},{3,4},{4,5},{5,6},{6,7},{7,8},{8,9},{9,10},{10,1... | collective-permute-start | bytes 786440 | tf_op jit(solution)/shard_map/ppermute | solution.py:14
  13.3 1.9 collective-permute-start.1
  16.6 1.7 fusion.73
  18.2 3.1 collective-permute-done.1
  27.6 3.2 collective-permute-start.2
  33.5 4.1 %collective-permute-start.3 = (bf16[2,4,64,256]{3,2,1,0:T(8,128)(2,1)S(1)}, bf16[2,4,64,256]{3,2,1,0:T(8,128)(2,1)S(1)}, u32[]{:S(2)}, u32[]{:S(2)}) collective-permute-start(bf16[2,4,64,256]{3,2,1,0:T(8,128)(2,1)S(1)} %slice.242), channel_id=1, source_target_pairs={{0,16},{16,32},{32,48},{48,64},{64,80},{80,96},{96,112},{112,128},... | collective-permute-start | bytes 786440 | tf_op jit(solution)/shard_map/ppermute | solution.py:25
  38.1 4.3 %collective-permute-done.3 = bf16[2,4,64,256]{3,2,1,0:T(8,128)(2,1)S(1)} collective-permute-done((bf16[2,4,64,256]{3,2,1,0:T(8,128)(2,1)S(1)}, bf16[2,4,64,256]{3,2,1,0:T(8,128)(2,1)S(1)}, u32[]{:S(2)}, u32[]{:S(2)}) %collective-permute-start.3) | collective-permute-done | bytes 262176 | tf_op jit(solution)/shard_map/ppermute | solution.py:25
  43.2 4.0 collective-permute-start.4
  48.1 10.5 %collective-permute-done.4 = bf16[4,4,64,256]{3,2,1,0:T(8,128)(2,1)S(1)} collective-permute-done((bf16[4,4,64,256]{3,2,1,0:T(8,128)(2,1)S(1)}, bf16[4,4,64,256]{3,2,1,0:T(8,128)(2,1)S(1)}, u32[]{:S(2)}, u32[]{:S(2)}) %collective-permute-start.4) | collective-permute-done | bytes 524320 | tf_op jit(solution)/shard_map/ppermute | solution.py:25
  62.2 4.7 %collective-permute-start.5 = (bf16[8,4,64,256]{3,2,1,0:T(8,128)(2,1)S(1)}, bf16[8,4,64,256]{3,2,1,0:T(8,128)(2,1)S(1)}, u32[]{:S(2)}, u32[]{:S(2)}) collective-permute-start(bf16[8,4,64,256]{3,2,1,0:T(8,128)(2,1)S(1)} %get-tuple-element.30), channel_id=1, source_target_pairs={{0,16},{16,32},{32,48},{48,64},{64,80},{80,96},{96,112},{112,128},... | collective-permute-start | bytes 3145736 | tf_op jit(solution)/shard_map/ppermute | solution.py:25
  68.4 8.3 %collective-permute-done.7 = bf16[4,4,64,256]{3,2,1,0:T(8,128)(2,1)S(1)} collective-permute-done((bf16[4,4,64,256]{3,2,1,0:T(8,128)(2,1)S(1)}, bf16[4,4,64,256]{3,2,1,0:T(8,128)(2,1)S(1)}, u32[]{:S(2)}, u32[]{:S(2)}) %collective-permute-start.7) | collective-permute-done | bytes 524320 | tf_op jit(solution)/shard_map/ppermute | solution.py:25
  80.7 6.8 %collective-permute-done.8 = bf16[2,4,64,256]{3,2,1,0:T(8,128)(2,1)S(1)} collective-permute-done((bf16[2,4,64,256]{3,2,1,0:T(8,128)(2,1)S(1)}, bf16[2,4,64,256]{3,2,1,0:T(8,128)(2,1)S(1)}, u32[]{:S(2)}, u32[]{:S(2)}) %collective-permute-start.8) | collective-permute-done | bytes 262176 | tf_op jit(solution)/shard_map/ppermute | solution.py:25
  91.4 5.3 %collective-permute-done.9 = bf16[1,4,64,256]{3,2,1,0:T(8,128)(2,1)S(1)} collective-permute-done((bf16[1,4,64,256]{3,2,1,0:T(8,128)(2,1)S(1)}, bf16[1,4,64,256]{3,2,1,0:T(8,128)(2,1)S(1)}, u32[]{:S(2)}, u32[]{:S(2)}) %collective-permute-start.9) | collective-permute-done | bytes 131104 | tf_op jit(solution)/shard_map/ppermute | solution.py:25
  102.2 1.6 pad_maximum_fusion
  103.7 3.1 copy.13
  111.6 5.0 %copy.12 = f32[9,256,256]{1,0,2:T(8,128)} copy(f32[9,256,256]{2,1,0:T(8,128)} %fusion.12) | data formatting | bytes 4718592 | tf_op jit(solution)/shard_map/stack | solution.py:112
  120.1 5.5 %collective-permute-start.11 = (bf16[8,1,64,256]{3,2,1,0:T(8,128)(2,1)S(1)}, bf16[8,1,64,256]{3,2,1,0:T(8,128)(2,1)S(1)}, u32[]{:S(2)}, u32[]{:S(2)}) collective-permute-start(bf16[8,1,64,256]{3,2,1,0:T(8,128)(2,1)S(1)} %get-tuple-element.14), channel_id=1, source_target_pairs={{1,0},{2,1},{3,2},{4,3},{5,4},{6,5},{7,6},{8,7},{9,8},{10,9},{11,1... | collective-permute-start | bytes 786440 | tf_op jit(solution)/shard_map/ppermute | solution.py:17
  125.6 1.9 collective-permute-start.10
  127.6 1.8 fusion.71
  129.4 2.3 add_convert_fusion.1
  131.7 1.8 fusion.2
  133.5 1.9 fusion.6
  136.3 1.9 fusion.23
  138.2 1.8 fusion.25
  140.0 1.8 fusion.27
  141.8 1.8 fusion.29
  143.7 1.9 fusion.31
  145.5 88.6 %all-reduce.7.cloned.1.call-done = f32[4,2,256,256]{2,0,1,3:T(4,128)} async-done(((f32[4,2,256,256]{2,0,1,3:T(4,128)}), f32[4,2,256,256]{2,0,1,3:T(4,128)}) %all-reduce.7.cloned.1.call-update) | async-done | bytes 2097168
  234.1 1.6 constant_dynamic-slice_fusion
  235.7 61.1 %reduce-scatter.2.cloned.1.call-done = f32[9,256,16]{1,0,2:T(8,128)} async-done(((f32[9,256,256]{1,0,2:T(8,128)}), f32[9,256,16]{1,0,2:T(8,128)}) %reduce-scatter.2.cloned.1.call-update) | async-done | bytes 147472 | tf_op jit(solution)/shard_map/reduce_scatter | solution.py:115
  296.8 7.8 %add_convert_fusion = bf16[8,4,64,256]{3,2,1,0:T(8,128)(2,1)} fusion(f32[8,4,64,256]{3,2,1,0:T(8,128)} %fusion.6, f32[8,4,64,256]{3,2,1,0:T(8,128)} %fusion.23, f32[8,4,64,256]{3,2,1,0:T(8,128)} %fusion.25, f32[8,4,64,256]{3,2,1,0:T(8,128)} %fusion.71, f32[8,4,64,256]{3,2,1,0:T(8,128)} %fusion.27, f32[8,4,64,256]{3,2,1,0:T(8,128)} %fusion.29, ...), kind=kOutput, calls=%fused_computation.4 | convolution fusion | flops 274202624 | bytes 20054016 | tf_op jit(solution)/shard_map/dot_general | solution.py:37
  304.7 90.7 %all-reduce.9.cloned.1.call-done = (f32[9,256,16]{1,0,2:T(8,128)}, f32[4,2,256,16]{2,0,1,3:T(4,128)}) async-done(((f32[9,256,16]{1,0,2:T(8,128)}, f32[4,2,256,16]{2,0,1,3:T(4,128)}), (f32[9,256,16]{1,0,2:T(8,128)}, f32[4,2,256,16]{2,0,1,3:T(4,128)})) %all-reduce.9.cloned.1.call-update) | async-done | bytes 278544 | tf_op jit(solution)/shard_map/psum | solution.py:113
  (114 shorter events, 43.6 us)
Async XLA Ops:
  7.2 14.2 %copy-start = (bf16[8,4,64,256]{3,2,1,0:T(8,128)(2,1)S(1)}, bf16[8,4,64,256]{3,2,1,0:T(8,128)(2,1)}, u32[]{:S(2)}) copy-start(bf16[8,4,64,256]{3,2,1,0:T(8,128)(2,1)} %param.4) | copy-start | bytes 3145732
  7.2 226.9 %all-reduce.7.cloned.1.call-start = ((), (), s32[]{:S(2)}) async-start(), calls=%async_computation.2 | async-start | bytes 4194304
  8.4 9.8 %collective-permute-start = (bf16[8,1,64,256]{3,2,1,0:T(8,128)(2,1)S(1)}, bf16[8,1,64,256]{3,2,1,0:T(8,128)(2,1)S(1)}, u32[]{:S(2)}, u32[]{:S(2)}) collective-permute-start(bf16[8,1,64,256]{3,2,1,0:T(8,128)(2,1)S(1)} %get-tuple-element.22), channel_id=1, source_target_pairs={{0,1},{1,2},{2,3},{3,4},{4,5},{5,6},{6,7},{7,8},{8,9},{9,10},{10,1... | collective-permute-start | bytes 786440 | tf_op jit(solution)/shard_map/ppermute | solution.py:14
  13.3 8.0 %collective-permute-start.1 = (bf16[8,1,64,256]{3,2,1,0:T(8,128)(2,1)S(1)}, bf16[8,1,64,256]{3,2,1,0:T(8,128)(2,1)S(1)}, u32[]{:S(2)}, u32[]{:S(2)}) collective-permute-start(bf16[8,1,64,256]{3,2,1,0:T(8,128)(2,1)S(1)} %get-tuple-element.23), channel_id=1, source_target_pairs={{1,0},{2,1},{3,2},{4,3},{5,4},{6,5},{7,6},{8,7},{9,8},{10,9},{11,1... | collective-permute-start | bytes 786440 | tf_op jit(solution)/shard_map/ppermute | solution.py:17
  15.3 44.1 %collective-permute-start.6 = (bf16[8,4,64,256]{3,2,1,0:T(8,128)(2,1)}, bf16[8,4,64,256]{3,2,1,0:T(8,128)(2,1)S(1)}, u32[]{:S(2)}, u32[]{:S(2)}) collective-permute-start(bf16[8,4,64,256]{3,2,1,0:T(8,128)(2,1)} %param.5), channel_id=1, source_target_pairs={{16,0},{32,16},{48,32},{64,48},{80,64},{96,80},{112,96},{128,112},... | collective-permute-start | bytes 3145736 | tf_op jit(solution)/shard_map/ppermute | solution.py:25
  18.2 4.0 copy-start.7
  24.7 1.1 copy-start.5
  26.2 4.6 %copy-start.14 = (bf16[4,2,256,256]{3,2,1,0:T(8,128)(2,1)S(1)}, bf16[4,2,256,256]{3,2,1,0:T(8,128)(2,1)}, u32[]{:S(2)}) copy-start(bf16[4,2,256,256]{3,2,1,0:T(8,128)(2,1)} %param.7) | copy-start | bytes 3145732
  27.6 5.1 %collective-permute-start.2 = (bf16[1,4,64,256]{3,2,1,0:T(8,128)(2,1)S(1)}, bf16[1,4,64,256]{3,2,1,0:T(8,128)(2,1)S(1)}, u32[]{:S(2)}, u32[]{:S(2)}) collective-permute-start(bf16[1,4,64,256]{3,2,1,0:T(8,128)(2,1)S(1)} %slice.240), channel_id=1, source_target_pairs={{0,16},{16,32},{32,48},{48,64},{64,80},{80,96},{96,112},{112,128},... | collective-permute-start | bytes 393224 | tf_op jit(solution)/shard_map/ppermute | solution.py:25
  33.5 8.8 %collective-permute-start.3 = (bf16[2,4,64,256]{3,2,1,0:T(8,128)(2,1)S(1)}, bf16[2,4,64,256]{3,2,1,0:T(8,128)(2,1)S(1)}, u32[]{:S(2)}, u32[]{:S(2)}) collective-permute-start(bf16[2,4,64,256]{3,2,1,0:T(8,128)(2,1)S(1)} %slice.242), channel_id=1, source_target_pairs={{0,16},{16,32},{32,48},{48,64},{64,80},{80,96},{96,112},{112,128},... | collective-permute-start | bytes 786440 | tf_op jit(solution)/shard_map/ppermute | solution.py:25
  43.1 4.1 %copy-start.3 = (bf16[8,4,64,256]{3,2,1,0:T(8,128)(2,1)S(1)}, bf16[8,4,64,256]{3,2,1,0:T(8,128)(2,1)}, u32[]{:S(2)}) copy-start(bf16[8,4,64,256]{3,2,1,0:T(8,128)(2,1)} %param.5) | copy-start | bytes 3145732
  43.2 15.4 %collective-permute-start.4 = (bf16[4,4,64,256]{3,2,1,0:T(8,128)(2,1)S(1)}, bf16[4,4,64,256]{3,2,1,0:T(8,128)(2,1)S(1)}, u32[]{:S(2)}, u32[]{:S(2)}) collective-permute-start(bf16[4,4,64,256]{3,2,1,0:T(8,128)(2,1)S(1)} %get-tuple-element.18), channel_id=1, source_target_pairs={{0,16},{16,32},{32,48},{48,64},{64,80},{80,96},{96,112},{112,128},... | collective-permute-start | bytes 1572872 | tf_op jit(solution)/shard_map/ppermute | solution.py:25
  59.3 8.2 %copy-start.9 = (bf16[8,4,64,256]{3,2,1,0:T(8,128)(2,1)}, bf16[8,4,64,256]{3,2,1,0:T(8,128)(2,1)S(1)}, u32[]{:S(2)}) copy-start(bf16[8,4,64,256]{3,2,1,0:T(8,128)(2,1)S(1)} %get-tuple-element.30) | copy-start | bytes 3145732
  60.9 15.8 %collective-permute-start.7 = (bf16[4,4,64,256]{3,2,1,0:T(8,128)(2,1)S(1)}, bf16[4,4,64,256]{3,2,1,0:T(8,128)(2,1)S(1)}, u32[]{:S(2)}, u32[]{:S(2)}) collective-permute-start(bf16[4,4,64,256]{3,2,1,0:T(8,128)(2,1)S(1)} %get-tuple-element.17), channel_id=1, source_target_pairs={{16,0},{32,16},{48,32},{64,48},{80,64},{96,80},{112,96},{128,112},... | collective-permute-start | bytes 1572872 | tf_op jit(solution)/shard_map/ppermute | solution.py:25
  62.2 38.2 %collective-permute-start.5 = (bf16[8,4,64,256]{3,2,1,0:T(8,128)(2,1)S(1)}, bf16[8,4,64,256]{3,2,1,0:T(8,128)(2,1)S(1)}, u32[]{:S(2)}, u32[]{:S(2)}) collective-permute-start(bf16[8,4,64,256]{3,2,1,0:T(8,128)(2,1)S(1)} %get-tuple-element.30), channel_id=1, source_target_pairs={{0,16},{16,32},{32,48},{48,64},{64,80},{80,96},{96,112},{112,128},... | collective-permute-start | bytes 3145736 | tf_op jit(solution)/shard_map/ppermute | solution.py:25
  78.3 9.1 %collective-permute-start.8 = (bf16[2,4,64,256]{3,2,1,0:T(8,128)(2,1)S(1)}, bf16[2,4,64,256]{3,2,1,0:T(8,128)(2,1)S(1)}, u32[]{:S(2)}, u32[]{:S(2)}) collective-permute-start(bf16[2,4,64,256]{3,2,1,0:T(8,128)(2,1)S(1)} %slice.249), channel_id=1, source_target_pairs={{16,0},{32,16},{48,32},{64,48},{80,64},{96,80},{112,96},{128,112},... | collective-permute-start | bytes 786440 | tf_op jit(solution)/shard_map/ppermute | solution.py:25
  89.5 7.2 %collective-permute-start.9 = (bf16[1,4,64,256]{3,2,1,0:T(8,128)(2,1)S(1)}, bf16[1,4,64,256]{3,2,1,0:T(8,128)(2,1)S(1)}, u32[]{:S(2)}, u32[]{:S(2)}) collective-permute-start(bf16[1,4,64,256]{3,2,1,0:T(8,128)(2,1)S(1)} %slice.251), channel_id=1, source_target_pairs={{16,0},{32,16},{48,32},{64,48},{80,64},{96,80},{112,96},{128,112},... | collective-permute-start | bytes 393224 | tf_op jit(solution)/shard_map/ppermute | solution.py:25
  98.6 1.2 copy-start.1
  100.4 1.4 copy-start.13
  100.4 1.7 copy-start.11
  106.9 189.9 %reduce-scatter.2.cloned.1.call-start = ((), (), s32[]{:S(2)}) async-start(), calls=%async_computation.1 | async-start | bytes 4456448 | tf_op jit(solution)/shard_map/reduce_scatter | solution.py:115
  106.9 2.3 copy-start.6
  116.6 0.7 copy-start.15
  116.6 1.9 copy-start.10
  116.7 278.7 %all-reduce.9.cloned.1.call-start = ((), (), s32[]{:S(2)}) async-start(), calls=%async_computation.3 | async-start | bytes 786432 | tf_op jit(solution)/shard_map/psum | solution.py:113
  118.6 9.0 %copy-start.8 = (bf16[9,256,256]{2,1,0:T(8,128)(2,1)S(1)}, bf16[9,256,256]{2,1,0:T(8,128)(2,1)}, u32[]{:S(2)}) copy-start(bf16[9,256,256]{2,1,0:T(8,128)(2,1)} %param.6) | copy-start | bytes 3538948
  120.0 9.3 %copy-start.2 = (bf16[8,4,64,256]{3,2,1,0:T(8,128)(2,1)S(1)}, bf16[8,4,64,256]{3,2,1,0:T(8,128)(2,1)}, u32[]{:S(2)}) copy-start(bf16[8,4,64,256]{3,2,1,0:T(8,128)(2,1)} %param.4) | copy-start | bytes 3145732
  120.0 9.3 %copy-start.12 = (bf16[8,4,64,256]{3,2,1,0:T(8,128)(2,1)S(1)}, bf16[8,4,64,256]{3,2,1,0:T(8,128)(2,1)}, u32[]{:S(2)}) copy-start(bf16[8,4,64,256]{3,2,1,0:T(8,128)(2,1)} %copy-done.11) | copy-start | bytes 3145732
  120.1 11.6 %collective-permute-start.11 = (bf16[8,1,64,256]{3,2,1,0:T(8,128)(2,1)S(1)}, bf16[8,1,64,256]{3,2,1,0:T(8,128)(2,1)S(1)}, u32[]{:S(2)}, u32[]{:S(2)}) collective-permute-start(bf16[8,1,64,256]{3,2,1,0:T(8,128)(2,1)S(1)} %get-tuple-element.14), channel_id=1, source_target_pairs={{1,0},{2,1},{3,2},{4,3},{5,4},{6,5},{7,6},{8,7},{9,8},{10,9},{11,1... | collective-permute-start | bytes 786440 | tf_op jit(solution)/shard_map/ppermute | solution.py:17
  125.6 7.9 %collective-permute-start.10 = (bf16[8,1,64,256]{3,2,1,0:T(8,128)(2,1)S(1)}, bf16[8,1,64,256]{3,2,1,0:T(8,128)(2,1)S(1)}, u32[]{:S(2)}, u32[]{:S(2)}) collective-permute-start(bf16[8,1,64,256]{3,2,1,0:T(8,128)(2,1)S(1)} %get-tuple-element.15), channel_id=1, source_target_pairs={{0,1},{1,2},{2,3},{3,4},{4,5},{5,6},{6,7},{7,8},{8,9},{9,10},{10,1... | collective-permute-start | bytes 786440 | tf_op jit(solution)/shard_map/ppermute | solution.py:14
  143.7 153.2 %copy-start.4 = (bf16[8,4,64,256]{3,2,1,0:T(8,128)(2,1)S(1)}, bf16[8,4,64,256]{3,2,1,0:T(8,128)(2,1)}, u32[]{:S(2)}) copy-start(bf16[8,4,64,256]{3,2,1,0:T(8,128)(2,1)} %param.5) | copy-start | bytes 3145732
Sparse Core Ops, SparseCore 0:
  107.0 127.1 all-reduce.6
  236.7 60.0 reduce-scatter.1
  300.7 94.6 all-reduce.8
where the time goes:
time: 406 us; the launch traced here: 405 us
  waiting for transfers between devices  280 us (69%)
  matrix products  52.8 us (13%)
  starting transfers between devices  35.6 us (9%)
  local copies, waits for them, and re-layouts  16.3 us (4%)
  between operations  15 us (4%)
  other arithmetic  5.48 us (1%)
    psum x1, waiting for transfers between devices, shards(): summed = lax.psum((spatial_total, time_total), 'tm')  90.7 us
    unnamed x4, waiting for transfers between devices  88.6 us
    reduce_scatter x1, waiting for transfers between devices, shards(): lax.psum_scatter(summed[0], 'rows', scatter_dimension=2, tiled=True)  61.1 us
    ppermute x8, waiting for transfers between devices, passed_along(): return lax.ppermute(block, axis, route)  36.6 us
    dot_general x17, matrix products, project_back(): lax.dot_general(flat, weight, (((1,), (1,)), ((), ())), preferred_element...  28.4 us
    ppermute x8, starting transfers between devices, passed_along(): return lax.ppermute(block, axis, route)  21.1 us
    dot_general x17, matrix products, project(): jnp.dot(flat, weight, preferred_element_type=jnp.float32)  13.4 us
    dot_general x17, matrix products, contract_rows(): lax.dot_general(left_flat, right_flat, (((0,), (0,)), ((), ())), preferre...  11 us
  transfers between devices with their start and end apart: 15, of which 10 were waited for; matrix products, arithmetic and copies ran while one was open for 15% of the time, Pallas kernels for 0%

commit v1 on v0

v1 whole, which is shorter than its diff:
```python
import math

import jax
import jax.numpy as jnp
from jax import lax
from jax.experimental import pallas as pl
from jax.experimental.pallas import tpu as pltpu
from jax.sharding import PartitionSpec as P

MESH = pl.DeviceIdType.MESH
F = 8
N = 256
BF = jnp.bfloat16
F32 = jnp.float32


def dot(a, b):
    return lax.dot_general(a, b, (((1,), (0,)), ((), ())), preferred_element_type=F32)


def columns(v):
    wide = v.astype(F32)
    n = wide.shape[0]
    col = lax.rem(lax.broadcasted_iota(jnp.int32, wide.shape, 0), 64)
    left = jnp.where(col == 0, 0.0, pltpu.roll(wide, 1, 0)).astype(BF)
    right = jnp.where(col == 63, 0.0, pltpu.roll(wide, n - 1, 0)).astype(BF)
    return left, right


def kernel(
    lat, cot, ws, wt,
    out, gin, gs_out, gt_out,
    xs, ys, lat_lo, lat_hi, sd_lo, sd_hi,
    s0, s1, s2, s3, slope, d0, d1, d2, d3h, sd, dT, wsT, wtT,
    g_t, g_s, ra_t, ra_s, ma_t, ma_s, rb_t, rb_s, mb_t, mb_s, rc_t, rc_s, mc_t, mc_s,
    row_sem, tm_sem, a_sem, b_send, b_recv, c_send, c_recv, h_send, h_recv,
):
    t = lax.axis_index("tm")
    r = lax.axis_index("rows")
    z = r // 2
    c = lax.rem(r, 2)
    tm_next = lax.rem(t + 1, 16)
    tm_prev = lax.rem(t + 15, 16)
    r_next = lax.rem(r + 1, 16)
    r_prev = lax.rem(r + 15, 16)
    sibling = r + 1 - 2 * c
    far = lax.rem(r + 15 + 2 * c, 16)
    states = (s0, s1, s2, s3)
    deltas = (d0, d1, d2)
    factor = 1.0 / math.sqrt(524288.0)

    barrier = pltpu.get_barrier_semaphore()
    for k in range(1, 16):
        pl.semaphore_signal(barrier, inc=1, device_id=(lax.rem(t + k, 16), r), device_id_type=MESH)
    for k in range(1, 8):
        pl.semaphore_signal(
            barrier, inc=1, device_id=(t, lax.rem(r + 2 * k, 16)), device_id_type=MESH
        )
    pl.semaphore_signal(barrier, inc=1, device_id=(t, sibling), device_id_type=MESH)
    pl.semaphore_signal(barrier, inc=1, device_id=(t, far), device_id_type=MESH)
    pl.semaphore_wait(barrier, 24)

    def remote(src, dst, send, recv, device):
        return pltpu.make_async_remote_copy(
            src_ref=src, dst_ref=dst, send_sem=send, recv_sem=recv, device_id=device,
            device_id_type=MESH,
        )

    lat_up = remote(lat.at[:, 192:256], lat_lo, row_sem.at[0], row_sem.at[1], (t, r_next))
    lat_dn = remote(lat.at[:, 0:64], lat_hi, row_sem.at[2], row_sem.at[3], (t, r_prev))
    lat_up.start()
    lat_dn.start()
    cot_dn = remote(cot, d3h, tm_sem.at[0], tm_sem.at[1], (tm_prev, r))
    cot_dn.start()
    state_up = [
        remote(
            states[k].at[8 : 8 + 2**k], states[k].at[0 : 2**k],
            tm_sem.at[2 + 2 * k], tm_sem.at[3 + 2 * k], (tm_next, r),
        )
        for k in range(4)
    ]
    delta_dn = [
        remote(
            deltas[k].at[0 : 2**k], deltas[k].at[8 : 8 + 2**k],
            tm_sem.at[10 + 2 * k], tm_sem.at[11 + 2 * k], (tm_prev, r),
        )
        for k in range(3)
    ]

    @pl.loop(0, F)
    def _(f):
        v = lat[f]
        left, right = columns(v)
        xs[f, 64:320, 0:256] = left
        xs[f, 64:320, 256:512] = v
        xs[f, 64:320, 512:768] = right

    for i in range(3):
        for j in range(3):
            wsT[i, 256 * j : 256 * j + 256, :] = ws[i, 256 * j : 256 * j + 256, :].T

    @pl.loop(0, 4)
    def _(k):
        wtT[k, 0:256, :] = wt[k, 0:256, :].T
        wtT[k, 256:512, :] = wt[k, 256:512, :].T

    lat_up.wait()
    lat_dn.wait()

    @pl.when(r == 0)
    def _():
        lat_lo[...] = jnp.zeros_like(lat_lo)

    @pl.when(r == 15)
    def _():
        lat_hi[...] = jnp.zeros_like(lat_hi)

    @pl.loop(0, F)
    def _(f):
        for ref, at in ((lat_lo, 0), (lat_hi, 320)):
            v = ref[f]
            left, right = columns(v)
            xs[f, at : at + 64, 0:256] = left
            xs[f, at : at + 64, 256:512] = v
            xs[f, at : at + 64, 512:768] = right

    def activate(k, f, n, v):
        sigma = 0.5 + 0.5 * jnp.tanh(0.5 * v)
        state = v * sigma
        states[k][pl.ds(2**k + f, n)] = state.astype(BF).reshape(n, N, N)
        slope[k, pl.ds(f, n)] = (sigma + state * (1.0 - sigma)).reshape(n, N, N)

    def blocks(low, high, body):
        f = low
        if (high - low) >= 4 and (high - low) % 2 == 0:
            @pl.loop(low // 2 * 2, high, step=2)
            def _(g):
                body(g, 2)
            return
        while f < high:
            n = min(2, high - f)
            body(f, n)
            f += n

    @pl.loop(0, F // 2)
    def _(b):
        f = 2 * b
        cat = jnp.concatenate(
            [xs[pl.ds(f, 2), 64 * i : 64 * i + 256, :].reshape(512, 768) for i in range(3)], axis=1
        )
        activate(0, f, 2, dot(cat, ws[...].reshape(2304, 256)))

    state_up[0].start()

    def past(ref, at, n):
        return ref[pl.ds(at, n)].reshape(n * N, N)

    def temporal(k, f, n):
        cat = jnp.concatenate(
            [past(states[k], f + 2**k, n), past(states[k], f, n)], axis=1
        )
        return dot(cat, wt[k])

    def forward(k):
        def body(f, n):
            activate(k + 1, f, n, temporal(k, f, n))
        return body

    def arrived_state(k):
        state_up[k].wait()

        @pl.when(t == 0)
        def _():
            states[k][0 : 2**k] = jnp.zeros((2**k, N, N), BF)

    f0 = forward(0)
    blocks(2, 8, f0)
    state_up[1].start()
    f0(1, 1)
    f1 = forward(1)
    blocks(4, 8, f1)
    state_up[2].start()
    f1(3, 1)
    arrived_state(0)
    f0(0, 1)
    arrived_state(1)
    f1(0, 2)
    f1(2, 1)
    f2 = forward(2)
    blocks(4, 8, f2)
    arrived_state(2)
    blocks(0, 4, f2)
    state_up[3].start()

    def delta_of(k):
        def body(f, n):
            if k == 3:
                now, later = past(cot, f, n), past(d3h, f, n)
            else:
                now, later = past(deltas[k], f, n), past(deltas[k], f + 2**k, n)
            back = dot(jnp.concatenate([now, later], axis=1), wtT[k])
            value = (back * slope[k, pl.ds(f, n)].reshape(n * N, N)).astype(BF)
            target = sd if k == 0 else deltas[k - 1]
            target[pl.ds(f, n)] = value.reshape(n, N, N)
        return body

    def put(ref, tap, value):
        for part in range(16):
            ref[part % 2, part // 2, tap] = value[16 * part : 16 * part + 16].astype(BF)

    def time_grads(k):
        d = 2**k
        for f in range(F):
            src = cot if k == 3 else deltas[k]
            dT[0:256, 256 * f : 256 * f + 256] = src[f].T
            other = d3h[f] if k == 3 else deltas[k][f + d]
            dT[256:512, 256 * f : 256 * f + 256] = other.T
        both = dot(dT[...], states[k][d : d + F].reshape(2048, N))
        put(g_t, 2 * k, both[0:256])
        put(g_t, 2 * k + 1, both[256:512])

    def arrived_delta(k):
        copy = cot_dn if k == 3 else delta_dn[k]
        copy.wait()

        @pl.when(t == 15)
        def _():
            if k == 3:
                d3h[...] = jnp.zeros_like(d3h)
            else:
                deltas[k][8 : 8 + 2**k] = jnp.zeros((2**k, N, N), BF)

    b3, b2, b1, b0 = delta_of(3), delta_of(2), delta_of(1), delta_of(0)
    arrived_delta(3)
    blocks(0, 4, b3)
    delta_dn[2].start()
    blocks(4, 8, b3)
    b2(0, 2)
    delta_dn[1].start()
    b2(2, 2)
    b1(0, 2)
    delta_dn[0].start()
    time_grads(3)
    arrived_delta(2)
    blocks(4, 8, b2)
    time_grads(2)
    b1(2, 2)
    b1(4, 2)
    arrived_delta(1)
    b1(6, 2)
    time_grads(1)
    b0(0, 2)
    b0(2, 2)
    b0(4, 2)
    arrived_delta(0)
    b0(6, 2)

    sd_up = remote(sd.at[:, 192:256], sd_lo, row_sem.at[4], row_sem.at[5], (t, r_next))
    sd_dn = remote(sd.at[:, 0:64], sd_hi, row_sem.at[6], row_sem.at[7], (t, r_prev))
    sd_up.start()
    sd_dn.start()

    def core_copy(g, ra, at):
        return remote(g.at[1 - c], ra, a_sem.at[at], a_sem.at[at + 1], (t, sibling))

    a_t = core_copy(g_t, ra_t, 0)
    a_s = core_copy(g_s, ra_s, 2)

    def z_copies(ma, rb, group):
        return [
            remote(
                ma.at[lax.rem(z + k, 8)], rb.at[z], b_send.at[group, k], b_recv.at[group, z],
                (t, lax.rem(r + 2 * k, 16)),
            )
            for k in range(1, 8)
        ]

    def z_arrival(rb, group, k):
        source = lax.rem(z + 8 - k, 8)
        return remote(
            rb.at[source], rb.at[source], b_send.at[group, k], b_recv.at[group, source],
            (t, lax.rem(r + 16 - 2 * k, 16)),
        )

    def add_cores(copy, g, ra, ma, rb, group):
        copy.wait()

        @pl.loop(0, 8)
        def _(p):
            ma[p] = (g[c, p].astype(F32) + ra[p].astype(F32)).astype(BF)

        copies = z_copies(ma, rb, group)
        for k in (4, 3, 5, 2, 6, 1, 7):
            copies[k - 1].start()
        rb[z] = ma[z]
        return copies

    def add_z(copies, rb, mb, group):
        for k in range(1, 8):
            z_arrival(rb, group, k).wait_recv()
        total = rb[0].astype(F32)
        for p in range(1, 8):
            total = total + rb[p].astype(F32)
        mb[...] = total.astype(BF)
        for copy in copies:
            copy.wait_send()

    def to_owner(taps, mb, rc, group, first):
        for k in range(taps):
            owner = first + k

            @pl.when(t != owner)
            def _():
                remote(
                    mb.at[k], rc.at[t], c_send.at[group, k], c_recv.at[group, t], (owner, r)
                ).start()

    def own_sum(taps, mb, rc, mc, group, first):
        mine = t - first

        @pl.when((t >= first) & (t < first + taps))
        def _():
            rc[t] = mb[mine]
            for k in range(1, 16):
                source = lax.rem(t + k, 16)
                remote(
                    rc.at[source], rc.at[source], c_send.at[group, 0], c_recv.at[group, source],
                    (source, r),
                ).wait_recv()
            total = rc[0].astype(F32)
            for p in range(1, 16):
                total = total + rc[p].astype(F32)
            mc[mine] = total.astype(BF)
            for k in range(1, 16):
                remote(
                    mc.at[mine], mc.at[mine], h_send.at[group, k], h_recv.at[group, mine],
                    (lax.rem(t + k, 16), r),
                ).start()

    def finish(taps, mb, rc, mc, group, first, target):
        mine = t - first
        for k in range(taps):
            owner = first + k

            @pl.when(t != owner)
            def _():
                remote(
                    mb.at[k], rc.at[t], c_send.at[group, k], c_recv.at[group, t], (owner, r)
                ).wait_send()
                remote(
                    mc.at[k], mc.at[k], h_send.at[group, 0], h_recv.at[group, k], (owner, r)
                ).wait_recv()

        target[...] = mc[...].astype(F32) * factor

        @pl.when((t >= first) & (t < first + taps))
        def _():
            for k in range(1, 16):
                remote(
                    mc.at[mine], mc.at[mine], h_send.at[group, k], h_recv.at[group, mine],
                    (lax.rem(t + k, 16), r),
                ).wait_send()

    time_grads(0)
    a_t.start()

    for f in range(F):
        dT[0:256, 256 * f : 256 * f + 256] = sd[f].T

    copies_t = None
    for i in range(3):
        for j in range(3):
            rows = xs[:, 64 * i : 64 * i + 256, 256 * j : 256 * j + 256].reshape(2048, N)
            put(g_s, 3 * i + j, dot(dT[0:256, :], rows))
        if i == 0:
            copies_t = add_cores(a_t, g_t, ra_t, ma_t, rb_t, 0)
    a_s.start()

    @pl.loop(0, F)
    def _(f):
        v = sd[f]
        left, right = columns(v)
        ys[f, 64:320, 0:256] = right
        ys[f, 64:320, 256:512] = v
        ys[f, 64:320, 512:768] = left

    sd_up.wait()
    sd_dn.wait()

    @pl.when(r == 0)
    def _():
        sd_lo[...] = jnp.zeros_like(sd_lo)

    @pl.when(r == 15)
    def _():
        sd_hi[...] = jnp.zeros_like(sd_hi)

    @pl.loop(0, F)
    def _(f):
        for ref, at in ((sd_lo, 0), (sd_hi, 320)):
            v = ref[f]
            left, right = columns(v)
            ys[f, at : at + 64, 0:256] = right
            ys[f, at : at + 64, 256:512] = v
            ys[f, at : at + 64, 512:768] = left

    copies_s = add_cores(a_s, g_s, ra_s, ma_s, rb_s, 1)
    add_z(copies_t, rb_t, mb_t, 0)
    to_owner(8, mb_t, rc_t, 0, 8)

    @pl.loop(0, F // 2)
    def _(b):
        f = 2 * b
        cat = jnp.concatenate(
            [
                ys[pl.ds(f, 2), 64 * (2 - i) : 64 * (2 - i) + 256, :].reshape(512, 768)
                for i in range(3)
            ],
            axis=1,
        )
        total = dot(cat, wsT[...].reshape(2304, 256)) + past(cot, f, 2).astype(F32)
        gin[pl.ds(f, 2)] = total.astype(BF).reshape(2, N, N)

    own_sum(8, mb_t, rc_t, mc_t, 0, 8)
    arrived_state(3)

    @pl.loop(0, F // 2)
    def _(b):
        f = 2 * b
        total = temporal(3, f, 2) + past(lat, f, 2).astype(F32)
        out[pl.ds(f, 2)] = total.astype(BF).reshape(2, N, N)

    add_z(copies_s, rb_s, mb_s, 1)
    to_owner(9, mb_s, rc_s, 1, 0)
    own_sum(9, mb_s, rc_s, mc_s, 1, 0)
    finish(8, mb_t, rc_t, mc_t, 0, 8, gt_out)
    finish(9, mb_s, rc_s, mc_s, 1, 0, gs_out)


def shards(latents, cotangent, w_spatial, w_time):
    shape = latents.shape
    vmem = pl.BlockSpec(memory_space=pltpu.VMEM)
    V = pltpu.VMEM
    scratch = [
        V((F, 384, 768), BF), V((F, 384, 768), BF),
        V((F, 64, N), BF), V((F, 64, N), BF), V((F, 64, N), BF), V((F, 64, N), BF),
        V((9, N, N), BF), V((10, N, N), BF), V((12, N, N), BF), V((16, N, N), BF),
        V((4, F, N, N), F32),
        V((9, N, N), BF), V((10, N, N), BF), V((12, N, N), BF), V((F, N, N), BF), V((F, N, N), BF),
        V((512, 2048), BF), V((3, 768, 256), BF), V((4, 512, 256), BF),
        V((2, 8, 8, 16, N), BF), V((2, 8, 9, 16, N), BF),
        V((8, 8, 16, N), BF), V((8, 9, 16, N), BF),
        V((8, 8, 16, N), BF), V((8, 9, 16, N), BF),
        V((8, 8, 16, N), BF), V((8, 9, 16, N), BF),
        V((8, 16, N), BF), V((9, 16, N), BF),
        V((16, 16, N), BF), V((16, 16, N), BF),
        V((8, 16, N), BF), V((9, 16, N), BF),
        pltpu.SemaphoreType.DMA((8,)), pltpu.SemaphoreType.DMA((16,)),
        pltpu.SemaphoreType.DMA((4,)),
        pltpu.SemaphoreType.DMA((2, 8)), pltpu.SemaphoreType.DMA((2, 8)),
        pltpu.SemaphoreType.DMA((2, 9)), pltpu.SemaphoreType.DMA((2, 16)),
        pltpu.SemaphoreType.DMA((2, 16)), pltpu.SemaphoreType.DMA((2, 9)),
    ]
    out, gin, gs, gt = pl.pallas_call(
        kernel,
        out_shape=[
            jax.ShapeDtypeStruct((F, N, N), BF),
            jax.ShapeDtypeStruct((F, N, N), BF),
            jax.ShapeDtypeStruct((9, 16, N), F32),
            jax.ShapeDtypeStruct((8, 16, N), F32),
        ],
        in_specs=[vmem] * 4,
        out_specs=[vmem] * 4,
        scratch_shapes=scratch,
        compiler_params=pltpu.CompilerParams(
            collective_id=0, has_side_effects=True, vmem_limit_bytes=60 * 1024 * 1024
        ),
        cost_estimate=pl.CostEstimate(
            flops=51 * 2 * 2048 * N * N, bytes_accessed=7 * 1024 * 1024, transcendentals=4 * 2048 * N
        ),
    )(
        latents.reshape(F, N, N), cotangent.reshape(F, N, N),
        w_spatial.reshape(3, 768, N), w_time.reshape(4, 512, N),
    )
    spatial = jnp.swapaxes(gs, 1, 2)
    time = jnp.swapaxes(gt, 1, 2).reshape(4, 2, N, 16)
    return out.reshape(shape), gin.reshape(shape), spatial, time


def solution(mesh):
    in_specs = (P("tm", "rows", None, None), P("tm", "rows", None, None), P(), P())
    out_specs = (
        P("tm", "rows", None, None),
        P("tm", "rows", None, None),
        P(None, None, "rows"),
        P(None, None, None, "rows"),
    )
    return jax.shard_map(shards, mesh=mesh, in_specs=in_specs, out_specs=out_specs, check_vma=False)
```

time: 406 us -> 114 us (0.28)
  waiting for transfers between devices: 280 us -> 0 us
  Pallas kernels: 0 us -> 108 us
  matrix products: 52.8 us -> 0 us
  starting transfers between devices: 35.6 us -> 0 us
  between operations: 15 us -> 0.65 us
  local copies, waits for them, and re-layouts: 16.3 us -> 4.74 us
  other arithmetic: 5.48 us -> 0 us
    pallas_call x0 -> x1, Pallas kernels: none -> 108 us  [shards(): pl.pallas_call(kernel, out_shape=[jax.ShapeDtypeStruct((F, N, N), BF), ja...]
    psum x1 -> x0, waiting for transfers between devices: 90.7 us -> none  [shards(): summed = lax.psum((spatial_total, time_total), 'tm')]
    unnamed x4 -> x0, waiting for transfers between devices: 88.6 us -> none
    reduce_scatter x1 -> x0, waiting for transfers between devices: 61.1 us -> none  [shards(): lax.psum_scatter(summed[0], 'rows', scatter_dimension=2, tiled=True)]
    dot_general x51 -> x0, matrix products: 52.8 us -> none  [the longest x17 28.4 us: project_back(): lax.dot_general(flat, weight, (((1,), (1,)), ((), ())), preferred_element...]
    ppermute x12 -> x0, waiting for transfers between devices: 39.7 us -> none  [the longest x8 36.6 us: passed_along(): return lax.ppermute(block, axis, route)]
    ppermute x12 -> x0, starting transfers between devices: 35.4 us -> none  [the longest x8 21.1 us: passed_along(): return lax.ppermute(block, axis, route)]
    another operation x2 -> x0, local copies, waits for them, and re-layouts: 8.12 us -> none  [the longest x1 5.02 us: shards(): spatial_total = jnp.stack(spatial_parts)]
  transfers between devices with their start and end apart: 15 -> 0, of which waited for: 10 -> 0; matrix products, arithmetic and copies ran while one was open for 15% -> 0% of each run, Pallas kernels for 0% -> 0%
where the time goes in v1:
time: 114 us
  Pallas kernels  108 us (95%)
  local copies, waits for them, and re-layouts  4.74 us (4%)
    pallas_call x1, Pallas kernels, shards(): pl.pallas_call(kernel, out_shape=[jax.ShapeDtypeStruct((F, N, N), BF), ja...  108 us
    unnamed x10, local copies, waits for them, and re-layouts  4.74 us

profile of v1, /device:TPU:1, one launch (start us, length us, event | category | flops | bytes accessed | tf_op | source)
XLA Modules:
  0.0 113.7 jit_solution(11043724418970071314)
XLA Ops:
  0.6 108.3 %shard_map.75 = (bf16[8,256,256]{2,1,0:T(8,128)(2,1)}, bf16[8,256,256]{2,1,0:T(8,128)(2,1)}, f32[9,16,256]{2,1,0:T(8,128)}, f32[8,16,256]{2,1,0:T(8,128)}) custom-call(bf16[8,256,256]{2,1,0:T(8,128)(2,1)} %bitcast.15, bf16[8,256,256]{2,1,0:T(8,128)(2,1)} %bitcast.16, bf16[3,768,256]{2,1,0:T(8,128)(2,1)} %bitcast.14, bf16[4,512,256]{2,1,0:T(8,128)(2,1)} %bitcast.17), custom_call_target="tpu_custom_call" | custom-call | flops 13690208256 | bytes 7340032 | tf_op jit(solution)/shard_map/pallas_call | solution.py:464
  108.9 0.0 copy-start
  109.0 2.4 %copy.12 = bf16[8,4,64,256]{3,2,1,0:T(8,128)(2,1)} copy(bf16[8,4,64,256]{3,2,1,0:T(8,128)(2,1)} %bitcast.11) | data formatting | bytes 2097152
  111.3 0.0 copy-done
  111.3 0.0 copy-start.1
  111.4 0.0 copy-start.2
  111.4 1.0 copy.13
  112.3 0.1 copy-done.1
  112.4 0.7 copy.14
  113.0 0.0 copy-done.2
  113.0 0.7 copy.15
Async XLA Ops:
  108.9 2.4 %copy-start = (bf16[8,256,256]{2,1,0:T(8,128)(2,1)S(1)}, bf16[8,256,256]{2,1,0:T(8,128)(2,1)}, u32[]{:S(2)}) copy-start(bf16[8,256,256]{2,1,0:T(8,128)(2,1)} %get-tuple-element.9) | copy-start | bytes 3145732
  111.3 1.0 copy-start.1
  111.4 1.7 %copy-start.2 = (f32[8,16,256]{2,1,0:T(8,128)S(1)}, f32[8,16,256]{2,1,0:T(8,128)}, u32[]{:S(2)}) copy-start(f32[8,16,256]{2,1,0:T(8,128)} %get-tuple-element.11) | copy-start | bytes 393220

commit v2 on v1

v2 whole, which is shorter than its diff:
```python
import math

import jax
import jax.numpy as jnp
from jax import lax
from jax.experimental import pallas as pl
from jax.experimental.pallas import tpu as pltpu
from jax.sharding import PartitionSpec as P

MESH = pl.DeviceIdType.MESH
F = 8
N = 256
HALF = 128
BF = jnp.bfloat16
F32 = jnp.float32


def dot(a, b):
    return lax.dot_general(a, b, (((1,), (0,)), ((), ())), preferred_element_type=F32)


def columns(v):
    wide = v.astype(F32)
    n = wide.shape[0]
    col = lax.rem(lax.broadcasted_iota(jnp.int32, wide.shape, 0), 64)
    left = jnp.where(col == 0, 0.0, pltpu.roll(wide, 1, 0)).astype(BF)
    right = jnp.where(col == 63, 0.0, pltpu.roll(wide, n - 1, 0)).astype(BF)
    return left, right


def kernel(
    lat_in, cot_in, ws_in, wt_in,
    out_hbm, gin_hbm, gs_out, gt_out,
    lat, cot, ws, wt, out, gin,
    xs, ys, lat_lo, lat_hi, sd_lo, sd_hi,
    s0, s1, s2, s3, slope, d0, d1, d2, d3h, sd, dT, wsT, wtT,
    g_a, g_b, g_x, g_y, g_z,
    ra_a, ra_b, ra_x, ra_y, ra_z,
    ma_a, ma_b, ma_x, ma_y, ma_z,
    rb_a, rb_b, rb_x, rb_y, rb_z,
    mb_t, mb_s, rc_t, rc_s, mc_t, mc_s,
    load_sem, row_sem, tm_send, tm_recv, a_sem, b_send, b_recv, c_send, c_recv, h_send, h_recv,
):
    t = lax.axis_index("tm")
    r = lax.axis_index("rows")
    z = r // 2
    c = lax.rem(r, 2)
    tm_next = lax.rem(t + 1, 16)
    tm_prev = lax.rem(t + 15, 16)
    r_next = lax.rem(r + 1, 16)
    r_prev = lax.rem(r + 15, 16)
    sibling = r + 1 - 2 * c
    far = lax.rem(r + 15 + 2 * c, 16)
    states = (s0, s1, s2, s3)
    deltas = (d0, d1, d2, d3h)
    factor = 1.0 / math.sqrt(524288.0)
    barrier = pltpu.get_barrier_semaphore()
    for k in (1, 15, 2, 14, 3, 13, 4, 12, 5, 11, 6, 10, 7, 9, 8):
        pl.semaphore_signal(barrier, inc=1, device_id=(lax.rem(t + k, 16), r), device_id_type=MESH)
    for k in range(1, 8):
        pl.semaphore_signal(
            barrier, inc=1, device_id=(t, lax.rem(r + 2 * k, 16)), device_id_type=MESH
        )
    pl.semaphore_signal(barrier, inc=1, device_id=(t, sibling), device_id_type=MESH)
    pl.semaphore_signal(barrier, inc=1, device_id=(t, far), device_id_type=MESH)

    loads = [
        pltpu.make_async_copy(src, dst, load_sem.at[k])
        for k, (src, dst) in enumerate(((lat_in, lat), (ws_in, ws), (wt_in, wt), (cot_in, cot)))
    ]
    for copy in loads:
        copy.start()
    pl.semaphore_wait(barrier, 24)

    def remote(src, dst, send, recv, device):
        return pltpu.make_async_remote_copy(
            src_ref=src, dst_ref=dst, send_sem=send, recv_sem=recv, device_id=device,
            device_id_type=MESH,
        )
    lat_up = remote(lat_in.at[:, 192:256], lat_lo, row_sem.at[0], row_sem.at[1], (t, r_next))
    lat_dn = remote(lat_in.at[:, 0:64], lat_hi, row_sem.at[2], row_sem.at[3], (t, r_prev))
    lat_up.start()
    lat_dn.start()

    def half(q):
        return slice(HALF * q, HALF * q + HALF)

    state_up = [
        [
            remote(
                states[k].at[8 : 8 + 2**k, half(q)], states[k].at[0 : 2**k, half(q)],
                tm_send.at[q, k], tm_recv.at[q, k], (tm_next, r),
            )
            for k in range(4)
        ]
        for q in range(2)
    ]
    delta_dn = [
        [
            remote(
                deltas[k].at[0 : 2**k, half(q)], deltas[k].at[8 : 8 + 2**k, half(q)],
                tm_send.at[q, 4 + k], tm_recv.at[q, 4 + k], (tm_prev, r),
            )
            for k in range(3)
        ]
        + [
            remote(
                cot_in.at[:, half(q)], d3h.at[:, half(q)], tm_send.at[q, 7], tm_recv.at[q, 7],
                (tm_prev, r),
            )
        ]
        for q in range(2)
    ]
    delta_dn[0][3].start()
    delta_dn[1][3].start()

    loads[0].wait()

    @pl.loop(0, F)
    def _(f):
        v = lat[f]
        left, right = columns(v)
        xs[f, 64:320, 0:256] = left
        xs[f, 64:320, 256:512] = v
        xs[f, 64:320, 512:768] = right

    loads[1].wait()
    lat_up.wait()
    lat_dn.wait()

    @pl.when(r == 0)
    def _():
        lat_lo[...] = jnp.zeros_like(lat_lo)

    @pl.when(r == 15)
    def _():
        lat_hi[...] = jnp.zeros_like(lat_hi)

    @pl.loop(0, F)
    def _(f):
        for ref, at in ((lat_lo, 0), (lat_hi, 320)):
            v = ref[f]
            left, right = columns(v)
            xs[f, at : at + 64, 0:256] = left
            xs[f, at : at + 64, 256:512] = v
            xs[f, at : at + 64, 512:768] = right

    def activate(k, f, n, q, v):
        sigma = 0.5 + 0.5 * jnp.tanh(0.5 * v)
        state = v * sigma
        states[k][2**k + f : 2**k + f + n, half(q)] = state.astype(BF).reshape(n, HALF, N)
        slope[k, f : f + n, half(q)] = (sigma + state * (1.0 - sigma)).reshape(n, HALF, N)

    def conv(f, n, q):
        cat = jnp.concatenate(
            [
                xs[f : f + n, 64 * i + HALF * q : 64 * i + HALF * q + HALF, :].reshape(n * HALF, 768)
                for i in range(3)
            ],
            axis=1,
        )
        activate(0, f, n, q, dot(cat, ws[...].reshape(2304, 256)))

    def past(ref, at, n, q):
        return ref[at : at + n, half(q)].reshape(n * HALF, N)

    def temporal(k, f, n, q):
        cat = jnp.concatenate(
            [past(states[k], f + 2**k, n, q), past(states[k], f, n, q)], axis=1
        )
        return dot(cat, wt[k])

    def forward(k, f, n, q):
        activate(k + 1, f, n, q, temporal(k, f, n, q))

    def arrived_state(k, q):
        state_up[q][k].wait()

        @pl.when(t == 0)
        def _():
            states[k][0 : 2**k, half(q)] = jnp.zeros((2**k, HALF, N), BF)
    for q in range(2):
        conv(4, 4, q)
        state_up[q][0].start()
        conv(0, 4, q)
        if q == 0:
            loads[2].wait()
        forward(0, 4, 4, q)
        state_up[q][1].start()
        forward(0, 1, 3, q)
        forward(1, 4, 4, q)
        state_up[q][2].start()
        forward(1, 3, 1, q)
    for i in range(3):
        for j in range(3):
            wsT[i, 256 * j : 256 * j + 256, :] = ws[i, 256 * j : 256 * j + 256, :].T

    @pl.loop(0, 4)
    def _(k):
        wtT[k, 0:256, :] = wt[k, 0:256, :].T
        wtT[k, 256:512, :] = wt[k, 256:512, :].T

    loads[3].wait()

    def back(k, f, n, q):
        source = cot if k == 3 else deltas[k]
        later = past(d3h, f, n, q) if k == 3 else past(deltas[k], f + 2**k, n, q)
        total = dot(jnp.concatenate([past(source, f, n, q), later], axis=1), wtT[k])
        value = (total * past(slope.at[k], f, n, q)).astype(BF)
        target = sd if k == 0 else deltas[k - 1]
        target[f : f + n, half(q)] = value.reshape(n, HALF, N)

    def arrived_delta(k, q):
        delta_dn[q][k].wait()
        at = 0 if k == 3 else 8

        @pl.when(t == 15)
        def _():
            deltas[k][at : at + 2**k, half(q)] = jnp.zeros((2**k, HALF, N), BF)

    for q in range(2):
        arrived_state(0, q)
        forward(0, 0, 1, q)
        arrived_state(1, q)
        forward(1, 0, 3, q)
        forward(2, 4, 4, q)
        arrived_state(2, q)
        forward(2, 0, 4, q)
        state_up[q][3].start()
        arrived_delta(3, q)
        back(3, 0, 4, q)
        delta_dn[q][2].start()
        back(3, 4, 4, q)
        back(2, 0, 4, q)
        delta_dn[q][1].start()
        back(1, 0, 2, q)
        delta_dn[q][0].start()

    def put(ref, tap, value):
        for part in range(16):
            ref[part % 2, part // 2, tap] = value[16 * part : 16 * part + 16].astype(BF)

    def time_grads(k, ref, tap):
        d = 2**k
        for f in range(F):
            src = cot if k == 3 else deltas[k]
            dT[0:256, 256 * f : 256 * f + 256] = src[f].T
            other = d3h[f] if k == 3 else deltas[k][f + d]
            dT[256:512, 256 * f : 256 * f + 256] = other.T
        both = dot(dT[...], states[k][d : d + F].reshape(2048, N))
        put(ref, tap, both[0:256])
        put(ref, tap + 1, both[256:512])

    groups = [
        (g_a, ra_a, ma_a, rb_a), (g_b, ra_b, ma_b, rb_b),
        (g_x, ra_x, ma_x, rb_x), (g_y, ra_y, ma_y, rb_y), (g_z, ra_z, ma_z, rb_z),
    ]
    between = [
        remote(g.at[1 - c], ra, a_sem.at[n, 0], a_sem.at[n, 1], (t, sibling))
        for n, (g, ra, _, _) in enumerate(groups)
    ]

    def z_copies(n):
        _, _, ma, rb = groups[n]
        return [
            remote(
                ma.at[lax.rem(z + k, 8)], rb.at[z], b_send.at[n, k], b_recv.at[n, z],
                (t, lax.rem(r + 2 * k, 16)),
            )
            for k in (4, 3, 5, 2, 6, 1, 7)
        ]

    def add_cores(n):
        g, ra, ma, rb = groups[n]
        between[n].wait()

        @pl.loop(0, 8)
        def _(p):
            ma[p] = (g[c, p].astype(F32) + ra[p].astype(F32)).astype(BF)

        for copy in z_copies(n):
            copy.start()
        rb[z] = ma[z]

    def add_z(n, mb, at):
        taps = groups[n][0].shape[2]
        rb = groups[n][3]
        for k in range(1, 8):
            source = lax.rem(z + 8 - k, 8)
            remote(
                rb.at[source], rb.at[source], b_send.at[n, k], b_recv.at[n, source],
                (t, lax.rem(r + 16 - 2 * k, 16)),
            ).wait_recv()
        total = rb[0].astype(F32)
        for p in range(1, 8):
            total = total + rb[p].astype(F32)
        mb[at : at + taps] = total.astype(BF)

    def sent_z(n):
        for copy in z_copies(n):
            copy.wait_send()

    def to_owner(low, high, mb, rc, group, first):
        for k in range(low, high):
            owner = first + k

            @pl.when(t != owner)
            def _():
                remote(
                    mb.at[k], rc.at[t], c_send.at[group, k], c_recv.at[group, t], (owner, r)
                ).start()

    def own_sum(taps, mb, rc, mc, group, first):
        mine = t - first

        @pl.when((t >= first) & (t < first + taps))
        def _():
            rc[t] = mb[mine]
            for k in range(1, 16):
                source = lax.rem(t + k, 16)
                remote(
                    rc.at[source], rc.at[source], c_send.at[group, 0], c_recv.at[group, source],
                    (source, r),
                ).wait_recv()
            total = rc[0].astype(F32)
            for p in range(1, 16):
                total = total + rc[p].astype(F32)
            mc[mine] = total.astype(BF)
            for k in range(1, 16):
                remote(
                    mc.at[mine], mc.at[mine], h_send.at[group, k], h_recv.at[group, mine],
                    (lax.rem(t + k, 16), r),
                ).start()

    def finish(taps, mb, rc, mc, group, first, target):
        mine = t - first
        for k in range(taps):
            owner = first + k

            @pl.when(t != owner)
            def _():
                remote(
                    mb.at[k], rc.at[t], c_send.at[group, k], c_recv.at[group, t], (owner, r)
                ).wait_send()
                remote(
                    mc.at[k], mc.at[k], h_send.at[group, 0], h_recv.at[group, k], (owner, r)
                ).wait_recv()

        target[...] = mc[...].astype(F32) * factor

        @pl.when((t >= first) & (t < first + taps))
        def _():
            for k in range(1, 16):
                remote(
                    mc.at[mine], mc.at[mine], h_send.at[group, k], h_recv.at[group, mine],
                    (lax.rem(t + k, 16), r),
                ).wait_send()
    time_grads(3, g_a, 2)
    arrived_delta(2, 0)
    back(2, 4, 4, 0)
    back(1, 2, 2, 0)
    arrived_delta(1, 0)
    back(1, 4, 4, 0)
    back(0, 0, 4, 0)
    arrived_delta(0, 0)
    back(0, 4, 4, 0)
    sd_dn = remote(sd.at[:, 0:64], sd_hi, row_sem.at[6], row_sem.at[7], (t, r_prev))
    sd_dn.start()
    arrived_delta(2, 1)
    back(2, 4, 4, 1)
    time_grads(2, g_a, 0)
    between[0].start()
    back(1, 2, 2, 1)
    arrived_delta(1, 1)
    back(1, 4, 4, 1)
    back(0, 0, 4, 1)
    add_cores(0)
    arrived_delta(0, 1)
    back(0, 4, 4, 1)
    sd_up = remote(sd.at[:, 192:256], sd_lo, row_sem.at[4], row_sem.at[5], (t, r_next))
    sd_up.start()

    def spatial_grads(i, ref):
        rows = xs[:, 64 * i : 64 * i + 256, :].reshape(2048, 768)
        total = dot(dT[0:256, :], rows)
        for j in range(3):
            put(ref, j, total[:, 256 * j : 256 * j + 256])

    for f in range(F):
        dT[0:256, 256 * f : 256 * f + 256] = sd[f].T
    spatial_grads(0, g_x)
    between[2].start()
    spatial_grads(1, g_y)
    between[3].start()
    add_cores(2)
    spatial_grads(2, g_z)
    between[4].start()
    add_cores(3)
    time_grads(1, g_b, 2)
    add_cores(4)
    time_grads(0, g_b, 0)
    between[1].start()

    @pl.loop(0, F)
    def _(f):
        v = sd[f]
        left, right = columns(v)
        ys[f, 64:320, 0:256] = right
        ys[f, 64:320, 256:512] = v
        ys[f, 64:320, 512:768] = left

    add_cores(1)
    sd_up.wait()
    sd_dn.wait()

    @pl.when(r == 0)
    def _():
        sd_lo[...] = jnp.zeros_like(sd_lo)

    @pl.when(r == 15)
    def _():
        sd_hi[...] = jnp.zeros_like(sd_hi)

    @pl.loop(0, F)
    def _(f):
        for ref, at in ((sd_lo, 0), (sd_hi, 320)):
            v = ref[f]
            left, right = columns(v)
            ys[f, at : at + 64, 0:256] = right
            ys[f, at : at + 64, 256:512] = v
            ys[f, at : at + 64, 512:768] = left
    def input_grads(f, n, q):
        cat = jnp.concatenate(
            [
                ys[f : f + n, 64 * (2 - i) + HALF * q : 64 * (2 - i) + HALF * q + HALF, :].reshape(
                    n * HALF, 768
                )
                for i in range(3)
            ],
            axis=1,
        )
        total = dot(cat, wsT[...].reshape(2304, 256)) + past(cot, f, n, q).astype(F32)
        gin[f : f + n, half(q)] = total.astype(BF).reshape(n, HALF, N)

    def outputs(f, n, q):
        total = temporal(3, f, n, q) + past(lat, f, n, q).astype(F32)
        out[f : f + n, half(q)] = total.astype(BF).reshape(n, HALF, N)

    input_grads(0, 4, 0)
    input_grads(4, 4, 0)
    add_z(0, mb_t, 4)
    to_owner(4, 8, mb_t, rc_t, 0, 8)
    input_grads(0, 4, 1)
    input_grads(4, 4, 1)
    gin_store = pltpu.make_async_copy(gin, gin_hbm, load_sem.at[4])
    gin_store.start()
    add_z(2, mb_s, 0)
    to_owner(0, 3, mb_s, rc_s, 1, 0)
    for q in range(2):
        arrived_state(3, q)
        outputs(0, 4, q)
        outputs(4, 4, q)
    out_store = pltpu.make_async_copy(out, out_hbm, load_sem.at[5])
    out_store.start()
    add_z(3, mb_s, 3)
    to_owner(3, 6, mb_s, rc_s, 1, 0)
    add_z(4, mb_s, 6)
    to_owner(6, 9, mb_s, rc_s, 1, 0)
    add_z(1, mb_t, 0)
    to_owner(0, 4, mb_t, rc_t, 0, 8)
    own_sum(9, mb_s, rc_s, mc_s, 1, 0)
    own_sum(8, mb_t, rc_t, mc_t, 0, 8)
    for n in range(5):
        sent_z(n)
    finish(9, mb_s, rc_s, mc_s, 1, 0, gs_out)
    finish(8, mb_t, rc_t, mc_t, 0, 8, gt_out)
    gin_store.wait()
    out_store.wait()
def handed_on(*refs):
    sem = refs[-1]
    copies = [
        pltpu.make_async_copy(refs[k], refs[4 + k], sem.at[k]) for k in range(4)
    ]
    for copy in copies:
        copy.start()
    for copy in copies:
        copy.wait()


def shards(latents, cotangent, w_spatial, w_time):
    shape = latents.shape
    vmem = pl.BlockSpec(memory_space=pltpu.VMEM)
    hbm = pl.BlockSpec(memory_space=pl.ANY)
    V = pltpu.VMEM
    DMA = pltpu.SemaphoreType.DMA
    sizes = (4, 4, 3, 3, 3)
    scratch = [
        V((F, N, N), BF), V((F, N, N), BF), V((3, 768, N), BF), V((4, 512, N), BF),
        V((F, N, N), BF), V((F, N, N), BF),
        V((F, 384, 768), BF), V((F, 384, 768), BF),
        V((F, 64, N), BF), V((F, 64, N), BF), V((F, 64, N), BF), V((F, 64, N), BF),
        V((9, N, N), BF), V((10, N, N), BF), V((12, N, N), BF), V((16, N, N), BF),
        V((4, F, N, N), F32),
        V((9, N, N), BF), V((10, N, N), BF), V((12, N, N), BF), V((F, N, N), BF), V((F, N, N), BF),
        V((512, 2048), BF), V((3, 768, 256), BF), V((4, 512, 256), BF),
        *[V((2, 8, n, 16, N), BF) for n in sizes],
        *[V((8, n, 16, N), BF) for n in sizes],
        *[V((8, n, 16, N), BF) for n in sizes],
        *[V((8, n, 16, N), BF) for n in sizes],
        V((8, 16, N), BF), V((9, 16, N), BF),
        V((16, 16, N), BF), V((16, 16, N), BF),
        V((8, 16, N), BF), V((9, 16, N), BF),
        DMA((6,)), DMA((8,)), DMA((2, 8)), DMA((2, 8)), DMA((5, 2)),
        DMA((5, 8)), DMA((5, 8)), DMA((2, 9)), DMA((2, 16)), DMA((2, 16)), DMA((2, 9)),
    ]
    results = [
        jax.ShapeDtypeStruct((F, N, N), BF),
        jax.ShapeDtypeStruct((F, N, N), BF),
        jax.ShapeDtypeStruct((9, 16, N), F32),
        jax.ShapeDtypeStruct((8, 16, N), F32),
    ]
    held = pl.pallas_call(
        kernel,
        out_shape=results,
        in_specs=[hbm] * 4,
        out_specs=[hbm, hbm, vmem, vmem],
        scratch_shapes=scratch,
        compiler_params=pltpu.CompilerParams(
            collective_id=0, has_side_effects=True, vmem_limit_bytes=60 * 1024 * 1024
        ),
        cost_estimate=pl.CostEstimate(
            flops=51 * 2 * 2048 * N * N, bytes_accessed=7 * 1024 * 1024, transcendentals=4 * 2048 * N
        ),
    )(
        latents.reshape(F, N, N), cotangent.reshape(F, N, N),
        w_spatial.reshape(3, 768, N), w_time.reshape(4, 512, N),
    )
    out, gin, gs, gt = pl.pallas_call(
        handed_on,
        out_shape=results,
        in_specs=[hbm] * 4,
        out_specs=[hbm] * 4,
        scratch_shapes=[DMA((4,))],
        cost_estimate=pl.CostEstimate(flops=0, bytes_accessed=5 * 1024 * 1024, transcendentals=0),
    )(*held)
    spatial = jnp.swapaxes(gs, 1, 2)
    time = jnp.swapaxes(gt, 1, 2).reshape(4, 2, N, 16)
    return out.reshape(shape), gin.reshape(shape), spatial, time


def solution(mesh):
    in_specs = (P("tm", "rows", None, None), P("tm", "rows", None, None), P(), P())
    out_specs = (
        P("tm", "rows", None, None),
        P("tm", "rows", None, None),
        P(None, None, "rows"),
        P(None, None, None, "rows"),
    )
    return jax.shard_map(shards, mesh=mesh, in_specs=in_specs, out_specs=out_specs, check_vma=False)
```

time: 114 us -> 170 us (1.49)
  Pallas kernels: 108 us -> 169 us
  local copies, waits for them, and re-layouts: 4.74 us -> 0 us
    pallas_call x1 -> x2, Pallas kernels: 108 us -> 169 us  [the longest x1 95.8 us: shards(): pl.pallas_call(kernel, out_shape=results, in_specs=[hbm] * 4, out_specs=[...]
    unnamed x10 -> x0, local copies, waits for them, and re-layouts: 4.74 us -> none
where the time goes in v2:
time: 170 us
  Pallas kernels  169 us (99%)
    pallas_call x1, Pallas kernels, shards(): pl.pallas_call(kernel, out_shape=results, in_specs=[hbm] * 4, out_specs=[...  95.8 us
    pallas_call x1, Pallas kernels, shards(): pl.pallas_call(handed_on, out_shape=results, in_specs=[hbm] * 4, out_spec...  73.1 us

profile of v2, /device:TPU:1, one launch (start us, length us, event | category | flops | bytes accessed | tf_op | source)
XLA Modules:
  0.0 169.7 jit_solution(6474399634202068145)
XLA Ops:
  0.6 95.8 %shard_map.75 = (bf16[8,256,256]{2,1,0:T(8,128)(2,1)}, bf16[8,256,256]{2,1,0:T(8,128)(2,1)}, f32[9,16,256]{2,1,0:T(8,128)}, f32[8,16,256]{2,1,0:T(8,128)}) custom-call(bf16[8,256,256]{2,1,0:T(8,128)(2,1)} %bitcast.11, bf16[8,256,256]{2,1,0:T(8,128)(2,1)} %bitcast.12, bf16[3,768,256]{2,1,0:T(8,128)(2,1)} %bitcast.10, bf16[4,512,256]{2,1,0:T(8,128)(2,1)} %bitcast.13), custom_call_target="tpu_custom_call" | custom-call | flops 13690208256 | bytes 7340032 | tf_op jit(solution)/shard_map/pallas_call | solution.py:522
  96.5 73.1 %shard_map.76 = (bf16[8,256,256]{2,1,0:T(8,128)(2,1)}, bf16[8,256,256]{2,1,0:T(8,128)(2,1)}, f32[9,16,256]{2,1,0:T(8,128)}, f32[8,16,256]{2,1,0:T(8,128)}) custom-call(bf16[8,256,256]{2,1,0:T(8,128)(2,1)} %get-tuple-element.12.refs_0_, bf16[8,256,256]{2,1,0:T(8,128)(2,1)} %get-tuple-element.13.refs_1_, f32[9,16,256]{2,1,0:T(8,128)} %get-tuple-element.14.refs_2_, ...), custom_call_target="tpu_custom_call" | custom-call | bytes 5242880 | tf_op jit(solution)/shard_map/pallas_call | solution.py:538

commit v3 on v2

--- a/solution.py
+++ b/solution.py
@@ -478,12 +478,14 @@
     out_store.wait()
 def handed_on(*refs):
     sem = refs[-1]
-    copies = [
-        pltpu.make_async_copy(refs[k], refs[4 + k], sem.at[k]) for k in range(4)
-    ]
-    for copy in copies:
+    loads = [pltpu.make_async_copy(refs[k], refs[8 + k], sem.at[0, k]) for k in range(4)]
+    stores = [pltpu.make_async_copy(refs[8 + k], refs[4 + k], sem.at[1, k]) for k in range(4)]
+    for copy in loads:
         copy.start()
-    for copy in copies:
+    for load, store in zip(loads, stores):
+        load.wait()
+        store.start()
+    for copy in stores:
         copy.wait()
 
 
@@ -540,7 +542,7 @@
         out_shape=results,
         in_specs=[hbm] * 4,
         out_specs=[hbm] * 4,
-        scratch_shapes=[DMA((4,))],
+        scratch_shapes=[*[V(x.shape, x.dtype) for x in results], DMA((2, 4))],
         cost_estimate=pl.CostEstimate(flops=0, bytes_accessed=5 * 1024 * 1024, transcendentals=0),
     )(*held)
     spatial = jnp.swapaxes(gs, 1, 2)

time: 170 us -> 99.4 us (0.58)
  Pallas kernels: 169 us -> 98.5 us
    pallas_call x1, Pallas kernels: 73.1 us -> 2.69 us  [shards(): pl.pallas_call(handed_on, out_shape=results, in_specs=[hbm] * 4, out_spec...]
where the time goes in v3:
time: 99.4 us; the launch traced here: 99.3 us
  Pallas kernels  98.5 us (99%)
    pallas_call x1, Pallas kernels, shards(): pl.pallas_call(kernel, out_shape=results, in_specs=[hbm] * 4, out_specs=[...  95.8 us
    pallas_call x1, Pallas kernels, shards(): pl.pallas_call(handed_on, out_shape=results, in_specs=[hbm] * 4, out_spec...  2.69 us

profile of v3, /device:TPU:1, one launch (start us, length us, event | category | flops | bytes accessed | tf_op | source)
XLA Modules:
  0.0 99.3 jit_solution(8958297941526310871)
XLA Ops:
  0.6 95.8 %shard_map.75 = (bf16[8,256,256]{2,1,0:T(8,128)(2,1)}, bf16[8,256,256]{2,1,0:T(8,128)(2,1)}, f32[9,16,256]{2,1,0:T(8,128)}, f32[8,16,256]{2,1,0:T(8,128)}) custom-call(bf16[8,256,256]{2,1,0:T(8,128)(2,1)} %bitcast.11, bf16[8,256,256]{2,1,0:T(8,128)(2,1)} %bitcast.12, bf16[3,768,256]{2,1,0:T(8,128)(2,1)} %bitcast.10, bf16[4,512,256]{2,1,0:T(8,128)(2,1)} %bitcast.13), custom_call_target="tpu_custom_call" | custom-call | flops 13690208256 | bytes 7340032 | tf_op jit(solution)/shard_map/pallas_call | solution.py:524
  96.5 2.7 %shard_map.76 = (bf16[8,256,256]{2,1,0:T(8,128)(2,1)}, bf16[8,256,256]{2,1,0:T(8,128)(2,1)}, f32[9,16,256]{2,1,0:T(8,128)}, f32[8,16,256]{2,1,0:T(8,128)}) custom-call(bf16[8,256,256]{2,1,0:T(8,128)(2,1)} %get-tuple-element.12.refs_0_, bf16[8,256,256]{2,1,0:T(8,128)(2,1)} %get-tuple-element.13.refs_1_, f32[9,16,256]{2,1,0:T(8,128)} %get-tuple-element.14.refs_2_, ...), custom_call_target="tpu_custom_call" | custom-call | bytes 5242880 | tf_op jit(solution)/shard_map/pallas_call | solution.py:540

commit v4 on v3

--- a/solution.py
+++ b/solution.py
@@ -37,7 +37,10 @@
     g_a, g_b, g_x, g_y, g_z,
     ra_a, ra_b, ra_x, ra_y, ra_z,
     ma_a, ma_b, ma_x, ma_y, ma_z,
-    rb_a, rb_b, rb_x, rb_y, rb_z,
+    rp_a, rp_b, rp_x, rp_y, rp_z,
+    rm_a, rm_b, rm_x, rm_y, rm_z,
+    sp_a, sp_b, sp_x, sp_y, sp_z,
+    sm_a, sm_b, sm_x, sm_y, sm_z,
     mb_t, mb_s, rc_t, rc_s, mc_t, mc_s,
     load_sem, row_sem, tm_send, tm_recv, a_sem, b_send, b_recv, c_send, c_recv, h_send, h_recv,
 ):
@@ -57,9 +60,9 @@
     barrier = pltpu.get_barrier_semaphore()
     for k in (1, 15, 2, 14, 3, 13, 4, 12, 5, 11, 6, 10, 7, 9, 8):
         pl.semaphore_signal(barrier, inc=1, device_id=(lax.rem(t + k, 16), r), device_id_type=MESH)
-    for k in range(1, 8):
+    for k in (2, 14):
         pl.semaphore_signal(
-            barrier, inc=1, device_id=(t, lax.rem(r + 2 * k, 16)), device_id_type=MESH
+            barrier, inc=1, device_id=(t, lax.rem(r + k, 16)), device_id_type=MESH
         )
     pl.semaphore_signal(barrier, inc=1, device_id=(t, sibling), device_id_type=MESH)
     pl.semaphore_signal(barrier, inc=1, device_id=(t, far), device_id_type=MESH)
@@ -70,7 +73,7 @@
     ]
     for copy in loads:
         copy.start()
-    pl.semaphore_wait(barrier, 24)
+    pl.semaphore_wait(barrier, 19)
 
     def remote(src, dst, send, recv, device):
         return pltpu.make_async_remote_copy(
@@ -252,53 +255,69 @@
         put(ref, tap + 1, both[256:512])
 
     groups = [
-        (g_a, ra_a, ma_a, rb_a), (g_b, ra_b, ma_b, rb_b),
-        (g_x, ra_x, ma_x, rb_x), (g_y, ra_y, ma_y, rb_y), (g_z, ra_z, ma_z, rb_z),
+        (g_a, ra_a, ma_a, rp_a, rm_a, sp_a, sm_a),
+        (g_b, ra_b, ma_b, rp_b, rm_b, sp_b, sm_b),
+        (g_x, ra_x, ma_x, rp_x, rm_x, sp_x, sm_x),
+        (g_y, ra_y, ma_y, rp_y, rm_y, sp_y, sm_y),
+        (g_z, ra_z, ma_z, rp_z, rm_z, sp_z, sm_z),
     ]
     between = [
-        remote(g.at[1 - c], ra, a_sem.at[n, 0], a_sem.at[n, 1], (t, sibling))
-        for n, (g, ra, _, _) in enumerate(groups)
-    ]
-
-    def z_copies(n):
-        _, _, ma, rb = groups[n]
-        return [
-            remote(
-                ma.at[lax.rem(z + k, 8)], rb.at[z], b_send.at[n, k], b_recv.at[n, z],
-                (t, lax.rem(r + 2 * k, 16)),
-            )
-            for k in (4, 3, 5, 2, 6, 1, 7)
-        ]
+        remote(group[0].at[1 - c], group[1], a_sem.at[n, 0], a_sem.at[n, 1], (t, sibling))
+        for n, group in enumerate(groups)
+    ]
+
+    def upward(n, step):
+        _, _, ma, rp, _, sp, _ = groups[n]
+        source = ma.at[lax.rem(z + 4, 8)] if step == 0 else sp.at[step - 1]
+        return remote(
+            source, rp.at[step], b_send.at[n, step], b_recv.at[n, step],
+            (t, lax.rem(r + 2, 16)),
+        )
+
+    def downward(n, step):
+        _, _, ma, _, rm, _, sm = groups[n]
+        source = ma.at[lax.rem(z + 5, 8)] if step == 0 else sm.at[step - 1]
+        return remote(
+            source, rm.at[step], b_send.at[n, 4 + step], b_recv.at[n, 4 + step],
+            (t, lax.rem(r + 14, 16)),
+        )
 
     def add_cores(n):
-        g, ra, ma, rb = groups[n]
+        g, ra, ma = groups[n][:3]
         between[n].wait()
 
         @pl.loop(0, 8)
         def _(p):
             ma[p] = (g[c, p].astype(F32) + ra[p].astype(F32)).astype(BF)
 
-        for copy in z_copies(n):
-            copy.start()
-        rb[z] = ma[z]
+        upward(n, 0).start()
+        downward(n, 0).start()
+
+    def pass_on(n, step):
+        _, _, ma, rp, rm, sp, sm = groups[n]
+        upward(n, step - 1).wait_recv()
+        sp[step - 1] = (ma[lax.rem(z + 4 - step, 8)].astype(F32) + rp[step - 1].astype(F32)).astype(BF)
+        upward(n, step).start()
+        if step < 3:
+            downward(n, step - 1).wait_recv()
+            sm[step - 1] = (
+                ma[lax.rem(z + 5 + step, 8)].astype(F32) + rm[step - 1].astype(F32)
+            ).astype(BF)
+            downward(n, step).start()
 
     def add_z(n, mb, at):
-        taps = groups[n][0].shape[2]
-        rb = groups[n][3]
-        for k in range(1, 8):
-            source = lax.rem(z + 8 - k, 8)
-            remote(
-                rb.at[source], rb.at[source], b_send.at[n, k], b_recv.at[n, source],
-                (t, lax.rem(r + 16 - 2 * k, 16)),
-            ).wait_recv()
-        total = rb[0].astype(F32)
-        for p in range(1, 8):
-            total = total + rb[p].astype(F32)
+        _, _, ma, rp, rm, _, _ = groups[n]
+        taps = ma.shape[1]
+        upward(n, 3).wait_recv()
+        downward(n, 2).wait_recv()
+        total = ma[z].astype(F32) + rp[3].astype(F32) + rm[2].astype(F32)
         mb[at : at + taps] = total.astype(BF)
 
     def sent_z(n):
-        for copy in z_copies(n):
-            copy.wait_send()
+        for step in range(4):
+            upward(n, step).wait_send()
+        for step in range(3):
+            downward(n, step).wait_send()
 
     def to_owner(low, high, mb, rc, group, first):
         for k in range(low, high):
@@ -368,12 +387,13 @@
     sd_dn.start()
     arrived_delta(2, 1)
     back(2, 4, 4, 1)
+    back(1, 2, 2, 1)
     time_grads(2, g_a, 0)
     between[0].start()
-    back(1, 2, 2, 1)
     arrived_delta(1, 1)
     back(1, 4, 4, 1)
     back(0, 0, 4, 1)
+    time_grads(1, g_b, 2)
     add_cores(0)
     arrived_delta(0, 1)
     back(0, 4, 4, 1)
@@ -386,21 +406,27 @@
         for j in range(3):
             put(ref, j, total[:, 256 * j : 256 * j + 256])
 
+    time_grads(0, g_b, 0)
+    between[1].start()
+    pass_on(0, 1)
     for f in range(F):
         dT[0:256, 256 * f : 256 * f + 256] = sd[f].T
     spatial_grads(0, g_x)
     between[2].start()
+    pass_on(0, 2)
+    add_cores(1)
     spatial_grads(1, g_y)
     between[3].start()
     add_cores(2)
+    pass_on(0, 3)
+    pass_on(1, 1)
     spatial_grads(2, g_z)
     between[4].start()
     add_cores(3)
-    time_grads(1, g_b, 2)
-    add_cores(4)
-    time_grads(0, g_b, 0)
-    between[1].start()
-
+    pass_on(1, 2)
+    pass_on(2, 1)
+    add_z(0, mb_t, 4)
+    to_owner(4, 8, mb_t, rc_t, 0, 8)
     @pl.loop(0, F)
     def _(f):
         v = sd[f]
@@ -409,7 +435,10 @@
         ys[f, 64:320, 256:512] = v
         ys[f, 64:320, 512:768] = left
 
-    add_cores(1)
+    add_cores(4)
+    pass_on(1, 3)
+    pass_on(2, 2)
+    pass_on(3, 1)
     sd_up.wait()
     sd_dn.wait()
 
@@ -429,6 +458,12 @@
             ys[f, at : at + 64, 0:256] = right
             ys[f, at : at + 64, 256:512] = v
             ys[f, at : at + 64, 512:768] = left
+
+    pass_on(2, 3)
+    pass_on(3, 2)
+    pass_on(4, 1)
+    add_z(1, mb_t, 0)
+    to_owner(0, 4, mb_t, rc_t, 0, 8)
     def input_grads(f, n, q):
         cat = jnp.concatenate(
             [
@@ -447,33 +482,32 @@
         out[f : f + n, half(q)] = total.astype(BF).reshape(n, HALF, N)
 
     input_grads(0, 4, 0)
+    pass_on(3, 3)
+    pass_on(4, 2)
+    add_z(2, mb_s, 0)
+    to_owner(0, 3, mb_s, rc_s, 1, 0)
     input_grads(4, 4, 0)
-    add_z(0, mb_t, 4)
-    to_owner(4, 8, mb_t, rc_t, 0, 8)
+    pass_on(4, 3)
+    add_z(3, mb_s, 3)
+    to_owner(3, 6, mb_s, rc_s, 1, 0)
     input_grads(0, 4, 1)
+    add_z(4, mb_s, 6)
+    to_owner(6, 9, mb_s, rc_s, 1, 0)
+    own_sum(8, mb_t, rc_t, mc_t, 0, 8)
     input_grads(4, 4, 1)
     gin_store = pltpu.make_async_copy(gin, gin_hbm, load_sem.at[4])
     gin_store.start()
-    add_z(2, mb_s, 0)
-    to_owner(0, 3, mb_s, rc_s, 1, 0)
+    own_sum(9, mb_s, rc_s, mc_s, 1, 0)
     for q in range(2):
         arrived_state(3, q)
         outputs(0, 4, q)
         outputs(4, 4, q)
     out_store = pltpu.make_async_copy(out, out_hbm, load_sem.at[5])
     out_store.start()
-    add_z(3, mb_s, 3)
-    to_owner(3, 6, mb_s, rc_s, 1, 0)
-    add_z(4, mb_s, 6)
-    to_owner(6, 9, mb_s, rc_s, 1, 0)
-    add_z(1, mb_t, 0)
-    to_owner(0, 4, mb_t, rc_t, 0, 8)
-    own_sum(9, mb_s, rc_s, mc_s, 1, 0)
-    own_sum(8, mb_t, rc_t, mc_t, 0, 8)
     for n in range(5):
         sent_z(n)
+    finish(8, mb_t, rc_t, mc_t, 0, 8, gt_out)
     finish(9, mb_s, rc_s, mc_s, 1, 0, gs_out)
-    finish(8, mb_t, rc_t, mc_t, 0, 8, gt_out)
     gin_store.wait()
     out_store.wait()
 def handed_on(*refs):
@@ -508,7 +542,10 @@
         *[V((2, 8, n, 16, N), BF) for n in sizes],
         *[V((8, n, 16, N), BF) for n in sizes],
         *[V((8, n, 16, N), BF) for n in sizes],
-        *[V((8, n, 16, N), BF) for n in sizes],
+        *[V((4, n, 16, N), BF) for n in sizes],
+        *[V((3, n, 16, N), BF) for n in sizes],
+        *[V((3, n, 16, N), BF) for n in sizes],
+        *[V((2, n, 16, N), BF) for n in sizes],
         V((8, 16, N), BF), V((9, 16, N), BF),
         V((16, 16, N), BF), V((16, 16, N), BF),
         V((8, 16, N), BF), V((9, 16, N), BF),

time: 99.4 us -> 101 us (1.016)
  the two profiles are of different devices: /device:TPU:1 before, /device:TPU:8 now
where the time goes in v4:
time: 101 us
  Pallas kernels  100 us (99%)
    pallas_call x1, Pallas kernels, shards(): pl.pallas_call(kernel, out_shape=results, in_specs=[hbm] * 4, out_specs=[...  97.5 us
    pallas_call x1, Pallas kernels, shards(): pl.pallas_call(handed_on, out_shape=results, in_specs=[hbm] * 4, out_spec...  2.69 us

profile of v4, /device:TPU:8, one launch (start us, length us, event | category | flops | bytes accessed | tf_op | source)
XLA Modules:
  0.0 101.0 jit_solution(6053036416355572948)
XLA Ops:
  0.6 97.5 %shard_map.75 = (bf16[8,256,256]{2,1,0:T(8,128)(2,1)}, bf16[8,256,256]{2,1,0:T(8,128)(2,1)}, f32[9,16,256]{2,1,0:T(8,128)}, f32[8,16,256]{2,1,0:T(8,128)}) custom-call(bf16[8,256,256]{2,1,0:T(8,128)(2,1)} %bitcast.11, bf16[8,256,256]{2,1,0:T(8,128)(2,1)} %bitcast.12, bf16[3,768,256]{2,1,0:T(8,128)(2,1)} %bitcast.10, bf16[4,512,256]{2,1,0:T(8,128)(2,1)} %bitcast.13), custom_call_target="tpu_custom_call" | custom-call | flops 13690208256 | bytes 7340032 | tf_op jit(solution)/shard_map/pallas_call | solution.py:561
  98.2 2.7 %shard_map.76 = (bf16[8,256,256]{2,1,0:T(8,128)(2,1)}, bf16[8,256,256]{2,1,0:T(8,128)(2,1)}, f32[9,16,256]{2,1,0:T(8,128)}, f32[8,16,256]{2,1,0:T(8,128)}) custom-call(bf16[8,256,256]{2,1,0:T(8,128)(2,1)} %get-tuple-element.12.refs_0_, bf16[8,256,256]{2,1,0:T(8,128)(2,1)} %get-tuple-element.13.refs_1_, f32[9,16,256]{2,1,0:T(8,128)} %get-tuple-element.14.refs_2_, ...), custom_call_target="tpu_custom_call" | custom-call | bytes 5242880 | tf_op jit(solution)/shard_map/pallas_call | solution.py:577

commit v5 on v3

--- a/solution.py
+++ b/solution.py
@@ -34,10 +34,10 @@
     lat, cot, ws, wt, out, gin,
     xs, ys, lat_lo, lat_hi, sd_lo, sd_hi,
     s0, s1, s2, s3, slope, d0, d1, d2, d3h, sd, dT, wsT, wtT,
-    g_a, g_b, g_x, g_y, g_z,
-    ra_a, ra_b, ra_x, ra_y, ra_z,
-    ma_a, ma_b, ma_x, ma_y, ma_z,
-    rb_a, rb_b, rb_x, rb_y, rb_z,
+    g_0, g_1, g_2, g_3, g_x, g_y, g_z,
+    ra_0, ra_1, ra_2, ra_3, ra_x, ra_y, ra_z,
+    ma_0, ma_1, ma_2, ma_3, ma_x, ma_y, ma_z,
+    rb_0, rb_1, rb_2, rb_3, rb_x, rb_y, rb_z,
     mb_t, mb_s, rc_t, rc_s, mc_t, mc_s,
     load_sem, row_sem, tm_send, tm_recv, a_sem, b_send, b_recv, c_send, c_recv, h_send, h_recv,
 ):
@@ -252,8 +252,13 @@
         put(ref, tap + 1, both[256:512])
 
     groups = [
-        (g_a, ra_a, ma_a, rb_a), (g_b, ra_b, ma_b, rb_b),
-        (g_x, ra_x, ma_x, rb_x), (g_y, ra_y, ma_y, rb_y), (g_z, ra_z, ma_z, rb_z),
+        (g_0, ra_0, ma_0, rb_0),
+        (g_1, ra_1, ma_1, rb_1),
+        (g_2, ra_2, ma_2, rb_2),
+        (g_3, ra_3, ma_3, rb_3),
+        (g_x, ra_x, ma_x, rb_x),
+        (g_y, ra_y, ma_y, rb_y),
+        (g_z, ra_z, ma_z, rb_z),
     ]
     between = [
         remote(g.at[1 - c], ra, a_sem.at[n, 0], a_sem.at[n, 1], (t, sibling))
@@ -355,30 +360,37 @@
                     mc.at[mine], mc.at[mine], h_send.at[group, k], h_recv.at[group, mine],
                     (lax.rem(t + k, 16), r),
                 ).wait_send()
-    time_grads(3, g_a, 2)
+    time_grads(3, g_3, 0)
+    between[3].start()
     arrived_delta(2, 0)
     back(2, 4, 4, 0)
     back(1, 2, 2, 0)
     arrived_delta(1, 0)
     back(1, 4, 4, 0)
     back(0, 0, 4, 0)
+    add_cores(3)
     arrived_delta(0, 0)
     back(0, 4, 4, 0)
     sd_dn = remote(sd.at[:, 0:64], sd_hi, row_sem.at[6], row_sem.at[7], (t, r_prev))
     sd_dn.start()
     arrived_delta(2, 1)
     back(2, 4, 4, 1)
-    time_grads(2, g_a, 0)
-    between[0].start()
     back(1, 2, 2, 1)
+    time_grads(2, g_2, 0)
+    between[2].start()
     arrived_delta(1, 1)
     back(1, 4, 4, 1)
     back(0, 0, 4, 1)
-    add_cores(0)
+    time_grads(1, g_1, 0)
+    between[1].start()
+    add_cores(2)
     arrived_delta(0, 1)
     back(0, 4, 4, 1)
     sd_up = remote(sd.at[:, 192:256], sd_lo, row_sem.at[4], row_sem.at[5], (t, r_next))
     sd_up.start()
+    time_grads(0, g_0, 0)
+    between[0].start()
+    add_cores(1)
 
     def spatial_grads(i, ref):
         rows = xs[:, 64 * i : 64 * i + 256, :].reshape(2048, 768)
@@ -389,17 +401,14 @@
     for f in range(F):
         dT[0:256, 256 * f : 256 * f + 256] = sd[f].T
     spatial_grads(0, g_x)
-    between[2].start()
+    between[4].start()
     spatial_grads(1, g_y)
-    between[3].start()
-    add_cores(2)
+    between[5].start()
+    add_cores(0)
+    add_cores(4)
     spatial_grads(2, g_z)
-    between[4].start()
-    add_cores(3)
-    time_grads(1, g_b, 2)
-    add_cores(4)
-    time_grads(0, g_b, 0)
-    between[1].start()
+    between[6].start()
+    add_cores(5)
 
     @pl.loop(0, F)
     def _(f):
@@ -409,7 +418,7 @@
         ys[f, 64:320, 256:512] = v
         ys[f, 64:320, 512:768] = left
 
-    add_cores(1)
+    add_cores(6)
     sd_up.wait()
     sd_dn.wait()
 
@@ -448,38 +457,47 @@
 
     input_grads(0, 4, 0)
     input_grads(4, 4, 0)
-    add_z(0, mb_t, 4)
-    to_owner(4, 8, mb_t, rc_t, 0, 8)
     input_grads(0, 4, 1)
     input_grads(4, 4, 1)
     gin_store = pltpu.make_async_copy(gin, gin_hbm, load_sem.at[4])
     gin_store.start()
-    add_z(2, mb_s, 0)
+    for k in (3, 2, 1, 0):
+        add_z(k, mb_t, 2 * k)
+        to_owner(2 * k, 2 * k + 2, mb_t, rc_t, 0, 8)
+    arrived_state(3, 0)
+    outputs(0, 4, 0)
+    outputs(4, 4, 0)
+    add_z(4, mb_s, 0)
     to_owner(0, 3, mb_s, rc_s, 1, 0)
-    for q in range(2):
-        arrived_state(3, q)
-        outputs(0, 4, q)
-        outputs(4, 4, q)
+    own_sum(8, mb_t, rc_t, mc_t, 0, 8)
+    arrived_state(3, 1)
+    outputs(0, 4, 1)
+    outputs(4, 4, 1)
     out_store = pltpu.make_async_copy(out, out_hbm, load_sem.at[5])
     out_store.start()
-    add_z(3, mb_s, 3)
+    add_z(5, mb_s, 3)
     to_owner(3, 6, mb_s, rc_s, 1, 0)
-    add_z(4, mb_s, 6)
+    add_z(6, mb_s, 6)
     to_owner(6, 9, mb_s, rc_s, 1, 0)
-    add_z(1, mb_t, 0)
-    to_owner(0, 4, mb_t, rc_t, 0, 8)
     own_sum(9, mb_s, rc_s, mc_s, 1, 0)
-    own_sum(8, mb_t, rc_t, mc_t, 0, 8)
-    for n in range(5):
+    for n in range(7):
         sent_z(n)
+    finish(8, mb_t, rc_t, mc_t, 0, 8, gt_out)
     finish(9, mb_s, rc_s, mc_s, 1, 0, gs_out)
-    finish(8, mb_t, rc_t, mc_t, 0, 8, gt_out)
     gin_store.wait()
     out_store.wait()
 def handed_on(*refs):
     sem = refs[-1]
-    loads = [pltpu.make_async_copy(refs[k], refs[8 + k], sem.at[0, k]) for k in range(4)]
-    stores = [pltpu.make_async_copy(refs[8 + k], refs[4 + k], sem.at[1, k]) for k in range(4)]
+    parts = [(k, slice(2 * p, 2 * p + 2)) for k in (0, 1) for p in range(4)]
+    parts += [(2, slice(0, 9)), (3, slice(0, 8))]
+    loads = [
+        pltpu.make_async_copy(refs[k].at[at], refs[8 + k].at[at], sem.at[0, n])
+        for n, (k, at) in enumerate(parts)
+    ]
+    stores = [
+        pltpu.make_async_copy(refs[8 + k].at[at], refs[4 + k].at[at], sem.at[1, n])
+        for n, (k, at) in enumerate(parts)
+    ]
     for copy in loads:
         copy.start()
     for load, store in zip(loads, stores):
@@ -495,7 +513,7 @@
     hbm = pl.BlockSpec(memory_space=pl.ANY)
     V = pltpu.VMEM
     DMA = pltpu.SemaphoreType.DMA
-    sizes = (4, 4, 3, 3, 3)
+    sizes = (2, 2, 2, 2, 3, 3, 3)
     scratch = [
         V((F, N, N), BF), V((F, N, N), BF), V((3, 768, N), BF), V((4, 512, N), BF),
         V((F, N, N), BF), V((F, N, N), BF),
@@ -512,8 +530,8 @@
         V((8, 16, N), BF), V((9, 16, N), BF),
         V((16, 16, N), BF), V((16, 16, N), BF),
         V((8, 16, N), BF), V((9, 16, N), BF),
-        DMA((6,)), DMA((8,)), DMA((2, 8)), DMA((2, 8)), DMA((5, 2)),
-        DMA((5, 8)), DMA((5, 8)), DMA((2, 9)), DMA((2, 16)), DMA((2, 16)), DMA((2, 9)),
+        DMA((6,)), DMA((8,)), DMA((2, 8)), DMA((2, 8)), DMA((7, 2)),
+        DMA((7, 8)), DMA((7, 8)), DMA((2, 9)), DMA((2, 16)), DMA((2, 16)), DMA((2, 9)),
     ]
     results = [
         jax.ShapeDtypeStruct((F, N, N), BF),
@@ -542,7 +560,7 @@
         out_shape=results,
         in_specs=[hbm] * 4,
         out_specs=[hbm] * 4,
-        scratch_shapes=[*[V(x.shape, x.dtype) for x in results], DMA((2, 4))],
+        scratch_shapes=[*[V(x.shape, x.dtype) for x in results], DMA((2, 10))],
         cost_estimate=pl.CostEstimate(flops=0, bytes_accessed=5 * 1024 * 1024, transcendentals=0),
     )(*held)
     spatial = jnp.swapaxes(gs, 1, 2)

time: 99.4 us -> 96.4 us (0.970)
  Pallas kernels: 98.5 us -> 95.5 us
    pallas_call x1, Pallas kernels: 95.8 us -> 92.9 us  [shards(): pl.pallas_call(kernel, out_shape=results, in_specs=[hbm] * 4, out_specs=[...]
where the time goes in v5:
time: 96.4 us; the launch traced here: 96.3 us
  Pallas kernels  95.5 us (99%)
    pallas_call x1, Pallas kernels, shards(): pl.pallas_call(kernel, out_shape=results, in_specs=[hbm] * 4, out_specs=[...  92.9 us
    pallas_call x1, Pallas kernels, shards(): pl.pallas_call(handed_on, out_shape=results, in_specs=[hbm] * 4, out_spec...  2.52 us

profile of v5, /device:TPU:1, one launch (start us, length us, event | category | flops | bytes accessed | tf_op | source)
XLA Modules:
  0.0 96.3 jit_solution(3109442318205285268)
XLA Ops:
  0.6 92.9 %shard_map.75 = (bf16[8,256,256]{2,1,0:T(8,128)(2,1)}, bf16[8,256,256]{2,1,0:T(8,128)(2,1)}, f32[9,16,256]{2,1,0:T(8,128)}, f32[8,16,256]{2,1,0:T(8,128)}) custom-call(bf16[8,256,256]{2,1,0:T(8,128)(2,1)} %bitcast.11, bf16[8,256,256]{2,1,0:T(8,128)(2,1)} %bitcast.12, bf16[3,768,256]{2,1,0:T(8,128)(2,1)} %bitcast.10, bf16[4,512,256]{2,1,0:T(8,128)(2,1)} %bitcast.13), custom_call_target="tpu_custom_call" | custom-call | flops 13690208256 | bytes 7340032 | tf_op jit(solution)/shard_map/pallas_call | solution.py:542
  93.6 2.5 %shard_map.76 = (bf16[8,256,256]{2,1,0:T(8,128)(2,1)}, bf16[8,256,256]{2,1,0:T(8,128)(2,1)}, f32[9,16,256]{2,1,0:T(8,128)}, f32[8,16,256]{2,1,0:T(8,128)}) custom-call(bf16[8,256,256]{2,1,0:T(8,128)(2,1)} %get-tuple-element.12.refs_0_, bf16[8,256,256]{2,1,0:T(8,128)(2,1)} %get-tuple-element.13.refs_1_, f32[9,16,256]{2,1,0:T(8,128)} %get-tuple-element.14.refs_2_, ...), custom_call_target="tpu_custom_call" | custom-call | bytes 5242880 | tf_op jit(solution)/shard_map/pallas_call | solution.py:558

commit v6 on v5

--- a/solution.py
+++ b/solution.py
@@ -30,8 +30,8 @@
 
 def kernel(
     lat_in, cot_in, ws_in, wt_in,
-    out_hbm, gin_hbm, gs_out, gt_out,
-    lat, cot, ws, wt, out, gin,
+    out, gin, gs_out, gt_out,
+    lat, cot, ws, wt,
     xs, ys, lat_lo, lat_hi, sd_lo, sd_hi,
     s0, s1, s2, s3, slope, d0, d1, d2, d3h, sd, dT, wsT, wtT,
     g_0, g_1, g_2, g_3, g_x, g_y, g_z,
@@ -459,8 +459,6 @@
     input_grads(4, 4, 0)
     input_grads(0, 4, 1)
     input_grads(4, 4, 1)
-    gin_store = pltpu.make_async_copy(gin, gin_hbm, load_sem.at[4])
-    gin_store.start()
     for k in (3, 2, 1, 0):
         add_z(k, mb_t, 2 * k)
         to_owner(2 * k, 2 * k + 2, mb_t, rc_t, 0, 8)
@@ -473,8 +471,6 @@
     arrived_state(3, 1)
     outputs(0, 4, 1)
     outputs(4, 4, 1)
-    out_store = pltpu.make_async_copy(out, out_hbm, load_sem.at[5])
-    out_store.start()
     add_z(5, mb_s, 3)
     to_owner(3, 6, mb_s, rc_s, 1, 0)
     add_z(6, mb_s, 6)
@@ -484,25 +480,16 @@
         sent_z(n)
     finish(8, mb_t, rc_t, mc_t, 0, 8, gt_out)
     finish(9, mb_s, rc_s, mc_s, 1, 0, gs_out)
-    gin_store.wait()
-    out_store.wait()
 def handed_on(*refs):
     sem = refs[-1]
-    parts = [(k, slice(2 * p, 2 * p + 2)) for k in (0, 1) for p in range(4)]
+    parts = [(k, slice(4 * p, 4 * p + 4)) for k in (0, 1) for p in range(2)]
     parts += [(2, slice(0, 9)), (3, slice(0, 8))]
-    loads = [
-        pltpu.make_async_copy(refs[k].at[at], refs[8 + k].at[at], sem.at[0, n])
+    stores = [
+        pltpu.make_async_copy(refs[k].at[at], refs[4 + k].at[at], sem.at[n])
         for n, (k, at) in enumerate(parts)
     ]
-    stores = [
-        pltpu.make_async_copy(refs[8 + k].at[at], refs[4 + k].at[at], sem.at[1, n])
-        for n, (k, at) in enumerate(parts)
-    ]
-    for copy in loads:
+    for copy in stores:
         copy.start()
-    for load, store in zip(loads, stores):
-        load.wait()
-        store.start()
     for copy in stores:
         copy.wait()
 
@@ -516,7 +503,6 @@
     sizes = (2, 2, 2, 2, 3, 3, 3)
     scratch = [
         V((F, N, N), BF), V((F, N, N), BF), V((3, 768, N), BF), V((4, 512, N), BF),
-        V((F, N, N), BF), V((F, N, N), BF),
         V((F, 384, 768), BF), V((F, 384, 768), BF),
         V((F, 64, N), BF), V((F, 64, N), BF), V((F, 64, N), BF), V((F, 64, N), BF),
         V((9, N, N), BF), V((10, N, N), BF), V((12, N, N), BF), V((16, N, N), BF),
@@ -530,7 +516,7 @@
         V((8, 16, N), BF), V((9, 16, N), BF),
         V((16, 16, N), BF), V((16, 16, N), BF),
         V((8, 16, N), BF), V((9, 16, N), BF),
-        DMA((6,)), DMA((8,)), DMA((2, 8)), DMA((2, 8)), DMA((7, 2)),
+        DMA((4,)), DMA((8,)), DMA((2, 8)), DMA((2, 8)), DMA((7, 2)),
         DMA((7, 8)), DMA((7, 8)), DMA((2, 9)), DMA((2, 16)), DMA((2, 16)), DMA((2, 9)),
     ]
     results = [
@@ -541,12 +527,12 @@
     ]
     held = pl.pallas_call(
         kernel,
-        out_shape=results,
+        out_shape=[V(x.shape, x.dtype) for x in results],
         in_specs=[hbm] * 4,
-        out_specs=[hbm, hbm, vmem, vmem],
+        out_specs=[vmem] * 4,
         scratch_shapes=scratch,
         compiler_params=pltpu.CompilerParams(
-            collective_id=0, has_side_effects=True, vmem_limit_bytes=60 * 1024 * 1024
+            collective_id=0, has_side_effects=True, vmem_limit_bytes=57 * 1024 * 1024
         ),
         cost_estimate=pl.CostEstimate(
             flops=51 * 2 * 2048 * N * N, bytes_accessed=7 * 1024 * 1024, transcendentals=4 * 2048 * N
@@ -558,11 +544,11 @@
     out, gin, gs, gt = pl.pallas_call(
         handed_on,
         out_shape=results,
-        in_specs=[hbm] * 4,
+        in_specs=[vmem] * 4,
         out_specs=[hbm] * 4,
-        scratch_shapes=[*[V(x.shape, x.dtype) for x in results], DMA((2, 10))],
+        scratch_shapes=[DMA((6,))],
         cost_estimate=pl.CostEstimate(flops=0, bytes_accessed=5 * 1024 * 1024, transcendentals=0),
-    )(*held)
+    )(*[pltpu.with_memory_space_constraint(x, V) for x in held])
     spatial = jnp.swapaxes(gs, 1, 2)
     time = jnp.swapaxes(gt, 1, 2).reshape(4, 2, N, 16)
     return out.reshape(shape), gin.reshape(shape), spatial, time

time: 96.4 us -> 94.5 us (0.980)
  Pallas kernels: 95.5 us -> 93.6 us
    pallas_call x2, Pallas kernels: 95.5 us -> 93.6 us  [the longest x1 92.2 us: shards(): pl.pallas_call(kernel, out_shape=[V(x.shape, x.dtype) for x in results],...]
where the time goes in v6:
time: 94.5 us; the launch traced here: 94.4 us
  Pallas kernels  93.6 us (99%)
    pallas_call x1, Pallas kernels, shards(): pl.pallas_call(kernel, out_shape=[V(x.shape, x.dtype) for x in results],...  92.2 us

profile of v6, /device:TPU:1, one launch (start us, length us, event | category | flops | bytes accessed | tf_op | source)
XLA Modules:
  0.0 94.4 jit_solution(219027195682482129)
XLA Ops:
  0.6 92.2 %shard_map.75 = (bf16[8,256,256]{2,1,0:T(8,128)(2,1)S(1)}, bf16[8,256,256]{2,1,0:T(8,128)(2,1)S(1)}, f32[9,16,256]{2,1,0:T(8,128)S(1)}, f32[8,16,256]{2,1,0:T(8,128)S(1)}) custom-call(bf16[8,256,256]{2,1,0:T(8,128)(2,1)} %bitcast.11, bf16[8,256,256]{2,1,0:T(8,128)(2,1)} %bitcast.12, bf16[3,768,256]{2,1,0:T(8,128)(2,1)} %bitcast.10, bf16[4,512,256]{2,1,0:T(8,128)(2,1)} %bitcast.13), custom_call_target="tpu_custom_call" | custom-call | flops 13690208256 | bytes 7340032 | tf_op jit(solution)/shard_map/pallas_call | solution.py:528
  92.8 1.4 %shard_map.76 = (bf16[8,256,256]{2,1,0:T(8,128)(2,1)}, bf16[8,256,256]{2,1,0:T(8,128)(2,1)}, f32[9,16,256]{2,1,0:T(8,128)}, f32[8,16,256]{2,1,0:T(8,128)}) custom-call(bf16[8,256,256]{2,1,0:T(8,128)(2,1)S(1)} %get-tuple-element.12.refs_0_, bf16[8,256,256]{2,1,0:T(8,128)(2,1)S(1)} %get-tuple-element.13.refs_1_, f32[9,16,256]{2,1,0:T(8,128)S(1)} %get-tuple-element.14.refs_2_, ...), custom_call_target="tpu_custom_call" | custom-call | bytes 5242880 | tf_op jit(solution)/shard_map/pallas_call | solution.py:544

commit v7 on v6

--- a/solution.py
+++ b/solution.py
@@ -275,6 +275,38 @@
             for k in (4, 3, 5, 2, 6, 1, 7)
         ]
 
+    rings = (0, 1, 2)
+
+    def upward(n, step):
+        _, ra, ma, rb = groups[n]
+        source = ma.at[lax.rem(z + 4, 8)] if step == 0 else ra.at[step - 1]
+        return remote(
+            source, rb.at[step], b_send.at[n, step], b_recv.at[n, step],
+            (t, lax.rem(r + 2, 16)),
+        )
+
+    def downward(n, step):
+        _, ra, ma, rb = groups[n]
+        source = ma.at[lax.rem(z + 5, 8)] if step == 0 else ra.at[3 + step]
+        return remote(
+            source, rb.at[4 + step], b_send.at[n, 4 + step], b_recv.at[n, 4 + step],
+            (t, lax.rem(r + 14, 16)),
+        )
+
+    def pass_on(n, step):
+        _, ra, ma, rb = groups[n]
+        upward(n, step - 1).wait_recv()
+        ra[step - 1] = (
+            ma[lax.rem(z + 4 - step, 8)].astype(F32) + rb[step - 1].astype(F32)
+        ).astype(BF)
+        upward(n, step).start()
+        if step < 3:
+            downward(n, step - 1).wait_recv()
+            ra[3 + step] = (
+                ma[lax.rem(z + 5 + step, 8)].astype(F32) + rb[3 + step].astype(F32)
+            ).astype(BF)
+            downward(n, step).start()
+
     def add_cores(n):
         g, ra, ma, rb = groups[n]
         between[n].wait()
@@ -283,13 +315,23 @@
         def _(p):
             ma[p] = (g[c, p].astype(F32) + ra[p].astype(F32)).astype(BF)
 
+        if n in rings:
+            upward(n, 0).start()
+            downward(n, 0).start()
+            return
         for copy in z_copies(n):
             copy.start()
         rb[z] = ma[z]
 
     def add_z(n, mb, at):
         taps = groups[n][0].shape[2]
-        rb = groups[n][3]
+        ma, rb = groups[n][2:]
+        if n in rings:
+            upward(n, 3).wait_recv()
+            downward(n, 2).wait_recv()
+            total = ma[z].astype(F32) + rb[3].astype(F32) + rb[6].astype(F32)
+            mb[at : at + taps] = total.astype(BF)
+            return
         for k in range(1, 8):
             source = lax.rem(z + 8 - k, 8)
             remote(
@@ -302,6 +344,12 @@
         mb[at : at + taps] = total.astype(BF)
 
     def sent_z(n):
+        if n in rings:
+            for step in range(4):
+                upward(n, step).wait_send()
+            for step in range(3):
+                downward(n, step).wait_send()
+            return
         for copy in z_copies(n):
             copy.wait_send()
 
@@ -388,9 +436,9 @@
     back(0, 4, 4, 1)
     sd_up = remote(sd.at[:, 192:256], sd_lo, row_sem.at[4], row_sem.at[5], (t, r_next))
     sd_up.start()
+    add_cores(1)
     time_grads(0, g_0, 0)
     between[0].start()
-    add_cores(1)
 
     def spatial_grads(i, ref):
         rows = xs[:, 64 * i : 64 * i + 256, :].reshape(2048, 768)
@@ -406,8 +454,10 @@
     between[5].start()
     add_cores(0)
     add_cores(4)
+    pass_on(2, 1)
     spatial_grads(2, g_z)
     between[6].start()
+    pass_on(1, 1)
     add_cores(5)
 
     @pl.loop(0, F)
@@ -419,6 +469,9 @@
         ys[f, 64:320, 512:768] = left
 
     add_cores(6)
+    pass_on(2, 2)
+    pass_on(0, 1)
+    pass_on(1, 2)
     sd_up.wait()
     sd_dn.wait()
 
@@ -456,7 +509,11 @@
         out[f : f + n, half(q)] = total.astype(BF).reshape(n, HALF, N)
 
     input_grads(0, 4, 0)
+    pass_on(2, 3)
+    pass_on(0, 2)
+    pass_on(1, 3)
     input_grads(4, 4, 0)
+    pass_on(0, 3)
     input_grads(0, 4, 1)
     input_grads(4, 4, 1)
     for k in (3, 2, 1, 0):

time: 94.5 us -> 103 us (1.090)
  the two profiles are of different devices: /device:TPU:1 before, /device:TPU:4 now
where the time goes in v7:
time: 103 us; the launch traced here: 102 us
  Pallas kernels  102 us (99%)
    pallas_call x1, Pallas kernels, shards(): pl.pallas_call(kernel, out_shape=[V(x.shape, x.dtype) for x in results],...  100 us

profile of v7, /device:TPU:4, one launch (start us, length us, event | category | flops | bytes accessed | tf_op | source)
XLA Modules:
  0.0 102.5 jit_solution(14697421063147097056)
XLA Ops:
  0.6 100.2 %shard_map.75 = (bf16[8,256,256]{2,1,0:T(8,128)(2,1)S(1)}, bf16[8,256,256]{2,1,0:T(8,128)(2,1)S(1)}, f32[9,16,256]{2,1,0:T(8,128)S(1)}, f32[8,16,256]{2,1,0:T(8,128)S(1)}) custom-call(bf16[8,256,256]{2,1,0:T(8,128)(2,1)} %bitcast.11, bf16[8,256,256]{2,1,0:T(8,128)(2,1)} %bitcast.12, bf16[3,768,256]{2,1,0:T(8,128)(2,1)} %bitcast.10, bf16[4,512,256]{2,1,0:T(8,128)(2,1)} %bitcast.13), custom_call_target="tpu_custom_call" | custom-call | flops 13690208256 | bytes 7340032 | tf_op jit(solution)/shard_map/pallas_call | solution.py:585
  100.9 1.4 %shard_map.76 = (bf16[8,256,256]{2,1,0:T(8,128)(2,1)}, bf16[8,256,256]{2,1,0:T(8,128)(2,1)}, f32[9,16,256]{2,1,0:T(8,128)}, f32[8,16,256]{2,1,0:T(8,128)}) custom-call(bf16[8,256,256]{2,1,0:T(8,128)(2,1)S(1)} %get-tuple-element.12.refs_0_, bf16[8,256,256]{2,1,0:T(8,128)(2,1)S(1)} %get-tuple-element.13.refs_1_, f32[9,16,256]{2,1,0:T(8,128)S(1)} %get-tuple-element.14.refs_2_, ...), custom_call_target="tpu_custom_call" | custom-call | bytes 5242880 | tf_op jit(solution)/shard_map/pallas_call | solution.py:601

commit v8 on v6

--- a/solution.py
+++ b/solution.py
@@ -381,16 +381,16 @@
     arrived_delta(1, 1)
     back(1, 4, 4, 1)
     back(0, 0, 4, 1)
+    add_cores(2)
     time_grads(1, g_1, 0)
     between[1].start()
-    add_cores(2)
     arrived_delta(0, 1)
     back(0, 4, 4, 1)
     sd_up = remote(sd.at[:, 192:256], sd_lo, row_sem.at[4], row_sem.at[5], (t, r_next))
     sd_up.start()
+    add_cores(1)
     time_grads(0, g_0, 0)
     between[0].start()
-    add_cores(1)
 
     def spatial_grads(i, ref):
         rows = xs[:, 64 * i : 64 * i + 256, :].reshape(2048, 768)

time: 94.5 us -> 94.1 us (level)
  no operation moved by 1% of the time
where the time goes in v8:
time: 94.1 us; the launch traced here: 94 us
  Pallas kernels  93.2 us (99%)
    pallas_call x1, Pallas kernels, shards(): pl.pallas_call(kernel, out_shape=[V(x.shape, x.dtype) for x in results],...  91.8 us

profile of v8, /device:TPU:1, one launch (start us, length us, event | category | flops | bytes accessed | tf_op | source)
XLA Modules:
  0.0 94.0 jit_solution(17790627322666215237)
XLA Ops:
  0.6 91.8 %shard_map.75 = (bf16[8,256,256]{2,1,0:T(8,128)(2,1)S(1)}, bf16[8,256,256]{2,1,0:T(8,128)(2,1)S(1)}, f32[9,16,256]{2,1,0:T(8,128)S(1)}, f32[8,16,256]{2,1,0:T(8,128)S(1)}) custom-call(bf16[8,256,256]{2,1,0:T(8,128)(2,1)} %bitcast.11, bf16[8,256,256]{2,1,0:T(8,128)(2,1)} %bitcast.12, bf16[3,768,256]{2,1,0:T(8,128)(2,1)} %bitcast.10, bf16[4,512,256]{2,1,0:T(8,128)(2,1)} %bitcast.13), custom_call_target="tpu_custom_call" | custom-call | flops 13690208256 | bytes 7340032 | tf_op jit(solution)/shard_map/pallas_call | solution.py:528
  92.4 1.4 %shard_map.76 = (bf16[8,256,256]{2,1,0:T(8,128)(2,1)}, bf16[8,256,256]{2,1,0:T(8,128)(2,1)}, f32[9,16,256]{2,1,0:T(8,128)}, f32[8,16,256]{2,1,0:T(8,128)}) custom-call(bf16[8,256,256]{2,1,0:T(8,128)(2,1)S(1)} %get-tuple-element.12.refs_0_, bf16[8,256,256]{2,1,0:T(8,128)(2,1)S(1)} %get-tuple-element.13.refs_1_, f32[9,16,256]{2,1,0:T(8,128)S(1)} %get-tuple-element.14.refs_2_, ...), custom_call_target="tpu_custom_call" | custom-call | bytes 5242880 | tf_op jit(solution)/shard_map/pallas_call | solution.py:544
